TPU v7x, 32 devices: a whole 2x2x4 slice. The times are simulated.
32 devices in a mesh: member: 2 (over y), lon: 16 (over z, x, core).
Axes of the slice: x: 2, y: 2, z: 4, core: 2. Of those that a mesh axis runs over, the one named last changes fastest.
Arguments:
- increment: bfloat16 [137, 256, 384], P(None, ('member', 'lon')), parts along dimension 1, may hold values from -6 to 6
- kernels: float32 [5, 25], replicated, may hold values from -1.5 to 1.5
- covariance: bfloat16 [5, 16, 137, 137], replicated, may hold values from -16 to 16, as said below
- region: int32 [16, 3], replicated, may hold values from 0 to 15
Outputs:
- balanced: bfloat16 [137, 256, 384], P(None, ('member', 'lon')), parts along dimension 1
There are 2 independent parts, one for each index of `member`. A program takes and returns all parts, laid end to end along the dimension named above; an argument that names none is the same for every part. Nothing has to cross between parts.
Inputs may be any that keep to these rules, and one draw needn't show every extreme that they name: `region`: each entry names one of the 16 regional blocks. `covariance`: each matrix is full.
All inputs are finite; a program needn't handle non-finite values.
Results may differ from a plain program's by a relative error of at most 0.0058.
Values may be sent and summed in bfloat16 or wider, within the bound.
No kernel may reach another device: no remote copies, remote signals or barrier semaphores. Data moves between devices by JAX's collectives and lax.ppermute only.
A program may use at most 128 MiB of HBM per device.

v0:
```python
import jax
import jax.numpy as jnp
from jax import lax
from jax.sharding import PartitionSpec as P

LEVELS = 4
BANDS = 5
REG_ROWS = 128


def from_partner(block, axis, bit):
    count = lax.axis_size(axis)
    route = []
    for low in range(count):
        high = low | 1 << bit
        if high != low and high < count:
            route += [(low, high), (high, low)]
    return lax.ppermute(block, axis, route)


def padded_2(cells, sides, width):
    for axis, dim in sides:
        count = lax.axis_size(axis)
        head = lax.slice_in_dim(cells, 0, width, axis=dim)
        tail = lax.slice_in_dim(cells, cells.shape[dim] - width, cells.shape[dim], axis=dim)
        cells = jnp.concatenate(
            [
                lax.ppermute(tail, axis, [(i, (i + 1) % count) for i in range(count)]),
                cells,
                lax.ppermute(head, axis, [((i + 1) % count, i) for i in range(count)]),
            ],
            axis=dim,
        )
    return cells


def filter_padded(padded, weights):
    lon_count = padded.shape[1] - 4
    lat_count = padded.shape[2] - 4
    summed = jnp.zeros((padded.shape[0], lon_count, lat_count), jnp.float32)
    for row_shift in range(5):
        for col_shift in range(5):
            window = padded[:, row_shift : row_shift + lon_count, col_shift : col_shift + lat_count]
            summed = summed + weights[row_shift * 5 + col_shift] * window.astype(jnp.float32)
    return summed.astype(jnp.bfloat16)


def apply_blocks(filtered, matrices, region_row):
    outputs = []
    for block_index in range(filtered.shape[2] // REG_ROWS):
        region_pick = region_row[block_index]
        matrix = lax.dynamic_index_in_dim(matrices, region_pick, 0, keepdims=False)
        columns = filtered[:, :, block_index * REG_ROWS : (block_index + 1) * REG_ROWS]
        outputs.append(
            jnp.einsum("ab,bxr->axr", matrix, columns, preferred_element_type=jnp.float32)
        )
    return jnp.concatenate(outputs, axis=2)


def on_device(increment, kernels, covariance, region):
    own_region = lax.dynamic_index_in_dim(region, lax.axis_index("lon"), 0, keepdims=False)
    first_partner = from_partner(increment, "lon", 0)
    smooth = increment.astype(jnp.float32)
    paired = 0.5 * (smooth + first_partner.astype(jnp.float32))
    bands_list = [(smooth - paired).astype(jnp.bfloat16)]
    smooth = paired
    for tier_index in range(1, LEVELS):
        partner = from_partner(smooth, "lon", tier_index)
        paired = 0.5 * (smooth + partner)
        bands_list.append((smooth - paired).astype(jnp.bfloat16))
        smooth = paired
    bands_list.append(smooth.astype(jnp.bfloat16))
    padded_list = [padded_2(band_field, (("lon", 1),), 2) for band_field in bands_list]
    summed = jnp.zeros(increment.shape, jnp.float32)
    for band_index in range(BANDS):
        padded = jnp.pad(padded_list[band_index], ((0, 0), (0, 0), (2, 2)))
        filtered = filter_padded(padded, kernels[band_index])
        summed = summed + apply_blocks(filtered, covariance[band_index], own_region)
    return summed.astype(jnp.bfloat16)


def solution(mesh):
    placed = (P(None, ("member", "lon"), None), P(), P(), P())
    return jax.shard_map(
        on_device,
        mesh=mesh,
        in_specs=placed,
        out_specs=P(None, ("member", "lon"), None),
        check_vma=False,
    )
```

profile of v0, /device:TPU:0, one launch (start us, length us, event | category | flops | bytes accessed | tf_op | source)
XLA Modules:
  0.0 249.2 jit_solution(14061115525449146208)
XLA Ops:
  7.0 2.1 fusion.64
  9.1 1.5 fusion.1
  11.2 3.0 %collective-permute-start.3 = (f32[137,8,384]{2,1,0:T(8,128)S(1)}, f32[137,8,384]{2,1,0:T(8,128)S(1)}, u32[]{:S(2)}, u32[]{:S(2)}) collective-permute-start(f32[137,8,384]{2,1,0:T(8,128)S(1)} %copy.20), channel_id=1, source_target_pairs={{0,2},{2,0},{1,3},{3,1},{4,6},{6,4},{5,7},{7,5},{8,10},{10,8},{9,1... | collective-permute-start | bytes 5050376 | tf_op jit(solution)/shard_map/ppermute | solution.py:18
  17.8 0.7 fusion.59
  21.3 29.6 %collective-permute-done.3 = f32[137,8,384]{2,1,0:T(8,128)S(1)} collective-permute-done((f32[137,8,384]{2,1,0:T(8,128)S(1)}, f32[137,8,384]{2,1,0:T(8,128)S(1)}, u32[]{:S(2)}, u32[]{:S(2)}) %collective-permute-start.3) | collective-permute-done | bytes 1683488 | tf_op jit(solution)/shard_map/ppermute | solution.py:18
  51.6 4.4 %collective-permute-start.5 = (bf16[137,2,384]{2,0,1:T(8,128)(2,1)S(1)}, bf16[137,2,384]{2,0,1:T(8,128)(2,1)S(1)}, u32[]{:S(2)}, u32[]{:S(2)}) collective-permute-start(bf16[137,2,384]{2,0,1:T(8,128)(2,1)S(1)} %get-tuple-element.39), channel_id=1, source_target_pairs={{1,0},{2,1},{3,2},{4,3},{5,4},{6,5},{7,6},{8,7},{9,8},{10,9},{11,1... | collective-permute-start | bytes 631304 | tf_op jit(solution)/shard_map/ppermute | solution.py:30
  56.2 4.4 %collective-permute-start.2 = (bf16[137,2,384]{2,0,1:T(8,128)(2,1)S(1)}, bf16[137,2,384]{2,0,1:T(8,128)(2,1)S(1)}, u32[]{:S(2)}, u32[]{:S(2)}) collective-permute-start(bf16[137,2,384]{2,0,1:T(8,128)(2,1)S(1)} %get-tuple-element.41), channel_id=1, source_target_pairs={{1,0},{2,1},{3,2},{4,3},{5,4},{6,5},{7,6},{8,7},{9,8},{10,9},{11,1... | collective-permute-start | bytes 631304 | tf_op jit(solution)/shard_map/ppermute | solution.py:30
  61.3 1.1 select_maximum_fusion.6
  62.4 22.3 %add_convert_fusion.3 = bf16[137,8,384]{2,0,1:T(8,128)(2,1)S(1)} fusion(bf16[137,8,384]{2,0,1:T(8,128)(2,1)S(1)} %get-tuple-element.7, bf16[137,2,384]{2,0,1:T(8,128)(2,1)S(1)} %collective-permute-done.5, bf16[137,2,384]{2,0,1:T(8,128)(2,1)S(1)} %collective-permute-done.4, bf16[137,12,388]{2,0,1:T(8,128)(2,1)S(1)} %select_maximum_fusion.6, f32[]{:T(128)} %bitcast.60, ...), kind=kLoop, calls=%fused_computation.33 | loop fusion | flops 33248256 | bytes 18938980 | tf_op jit(solution)/shard_map/convert_element_type | solution.py:45
  85.2 1.1 select_maximum_fusion.8
  86.5 22.2 %add_convert_fusion.4 = bf16[137,8,384]{2,0,1:T(8,128)(2,1)S(1)} fusion(bf16[137,8,384]{2,0,1:T(8,128)(2,1)S(1)} %get-tuple-element.16, bf16[137,2,384]{2,0,1:T(8,128)(2,1)S(1)} %collective-permute-done.2, bf16[137,2,384]{2,0,1:T(8,128)(2,1)S(1)} %collective-permute-done.1, bf16[137,12,388]{2,0,1:T(8,128)(2,1)S(1)} %select_maximum_fusion.8, f32[]{:T(128)} %bitcast.27, ...), kind=kLoop, calls=%fused_computation.35 | loop fusion | flops 33248256 | bytes 18938980 | tf_op jit(solution)/shard_map/convert_element_type | solution.py:45
  109.9 4.7 %collective-permute-start.8 = (bf16[137,2,384]{2,0,1:T(8,128)(2,1)S(1)}, bf16[137,2,384]{2,0,1:T(8,128)(2,1)S(1)}, u32[]{:S(2)}, u32[]{:S(2)}) collective-permute-start(bf16[137,2,384]{2,0,1:T(8,128)(2,1)S(1)} %get-tuple-element.37), channel_id=1, source_target_pairs={{1,0},{2,1},{3,2},{4,3},{5,4},{6,5},{7,6},{8,7},{9,8},{10,9},{11,1... | collective-permute-start | bytes 631304 | tf_op jit(solution)/shard_map/ppermute | solution.py:30
  115.4 2.8 %collective-permute-done.7 = bf16[137,2,384]{2,0,1:T(8,128)(2,1)S(1)} collective-permute-done((bf16[137,2,384]{2,0,1:T(8,128)(2,1)S(1)}, bf16[137,2,384]{2,0,1:T(8,128)(2,1)S(1)}, u32[]{:S(2)}, u32[]{:S(2)}) %collective-permute-start.7) | collective-permute-done | bytes 210464 | tf_op jit(solution)/shard_map/ppermute | solution.py:28
  118.2 2.1 collective-permute-done.8
  120.4 1.1 select_maximum_fusion.4
  121.4 22.3 %add_convert_fusion.2 = bf16[137,8,384]{2,0,1:T(8,128)(2,1)S(1)} fusion(bf16[137,8,384]{2,0,1:T(8,128)(2,1)S(1)} %get-tuple-element.5, bf16[137,2,384]{2,0,1:T(8,128)(2,1)S(1)} %collective-permute-done.8, bf16[137,2,384]{2,0,1:T(8,128)(2,1)S(1)} %collective-permute-done.7, bf16[137,12,388]{2,0,1:T(8,128)(2,1)S(1)} %select_maximum_fusion.4, f32[]{:T(128)} %bitcast.91, ...), kind=kLoop, calls=%fused_computation.31 | loop fusion | flops 33248256 | bytes 18938980 | tf_op jit(solution)/shard_map/convert_element_type | solution.py:45
  144.4 45.6 %collective-permute-done.9 = f32[137,8,384]{2,1,0:T(8,128)S(1)} collective-permute-done((f32[137,8,384]{2,1,0:T(8,128)S(1)}, f32[137,8,384]{2,1,0:T(8,128)S(1)}, u32[]{:S(2)}, u32[]{:S(2)}) %collective-permute-start.9) | collective-permute-done | bytes 1683488 | tf_op jit(solution)/shard_map/ppermute | solution.py:18
  190.6 4.4 %collective-permute-start.11 = (bf16[137,2,384]{2,0,1:T(8,128)(2,1)S(1)}, bf16[137,2,384]{2,0,1:T(8,128)(2,1)S(1)}, u32[]{:S(2)}, u32[]{:S(2)}) collective-permute-start(bf16[137,2,384]{2,0,1:T(8,128)(2,1)S(1)} %get-tuple-element.35), channel_id=1, source_target_pairs={{1,0},{2,1},{3,2},{4,3},{5,4},{6,5},{7,6},{8,7},{9,8},{10,9},{11,1... | collective-permute-start | bytes 631304 | tf_op jit(solution)/shard_map/ppermute | solution.py:30
  195.1 4.4 %collective-permute-start.13 = (bf16[137,2,384]{2,0,1:T(8,128)(2,1)S(1)}, bf16[137,2,384]{2,0,1:T(8,128)(2,1)S(1)}, u32[]{:S(2)}, u32[]{:S(2)}) collective-permute-start(bf16[137,2,384]{2,0,1:T(8,128)(2,1)S(1)} %get-tuple-element.33), channel_id=1, source_target_pairs={{1,0},{2,1},{3,2},{4,3},{5,4},{6,5},{7,6},{8,7},{9,8},{10,9},{11,1... | collective-permute-start | bytes 631304 | tf_op jit(solution)/shard_map/ppermute | solution.py:30
  199.5 1.1 select_maximum_fusion.2
  200.6 22.3 %add_convert_fusion.1 = bf16[137,8,384]{2,0,1:T(8,128)(2,1)S(1)} fusion(bf16[137,8,384]{2,0,1:T(8,128)(2,1)S(1)} %get-tuple-element.15, bf16[137,2,384]{2,0,1:T(8,128)(2,1)S(1)} %collective-permute-done.11, bf16[137,2,384]{2,0,1:T(8,128)(2,1)S(1)} %collective-permute-done.10, bf16[137,12,388]{2,0,1:T(8,128)(2,1)S(1)} %select_maximum_fusion.2, f32[]{:T(128)} %bitcast.122, ...), kind=kLoop, calls=%fused_computation.29 | loop fusion | flops 33248256 | bytes 18938980 | tf_op jit(solution)/shard_map/convert_element_type | solution.py:45
  223.6 1.1 select_maximum_fusion
  224.6 22.3 %add_convert_fusion = bf16[137,8,384]{2,0,1:T(8,128)(2,1)S(1)} fusion(bf16[137,8,384]{2,0,1:T(8,128)(2,1)S(1)} %get-tuple-element.14, bf16[137,2,384]{2,0,1:T(8,128)(2,1)S(1)} %collective-permute-done.13, bf16[137,2,384]{2,0,1:T(8,128)(2,1)S(1)} %collective-permute-done.12, bf16[137,12,388]{2,0,1:T(8,128)(2,1)S(1)} %select_maximum_fusion, f32[]{:T(128)} %bitcast.153, ...), kind=kLoop, calls=%fused_computation.28 | loop fusion | flops 33248256 | bytes 18938980 | tf_op jit(solution)/shard_map/convert_element_type | solution.py:45
  248.2 1.1 copy.29
  (66 shorter events, 15.7 us)
Async XLA Ops:
  0.0 0.7 copy-start
  0.0 9.1 %collective-permute-start = (bf16[137,8,384]{2,1,0:T(8,128)(2,1)}, bf16[137,8,384]{2,1,0:T(8,128)(2,1)S(1)}, u32[]{:S(2)}, u32[]{:S(2)}) collective-permute-start(bf16[137,8,384]{2,1,0:T(8,128)(2,1)} %param.4), channel_id=1, source_target_pairs={{0,1},{1,0},{2,3},{3,2},{4,5},{5,4},{6,7},{7,6},{8,9},{9,8},{10,11... | collective-permute-start | bytes 2525192 | tf_op jit(solution)/shard_map/ppermute | solution.py:18
  9.1 9.4 %copy-start.1 = (bf16[5,16,137,137]{3,1,2,0:T(8,128)(2,1)S(1)}, bf16[5,16,137,137]{3,1,2,0:T(8,128)(2,1)}, u32[]{:S(2)}) copy-start(bf16[5,16,137,137]{3,1,2,0:T(8,128)(2,1)} %param.6) | copy-start | bytes 9009124
  10.6 3.6 %copy-start.3 = (f32[5,25]{1,0:T(8,128)S(1)}, f32[5,25]{1,0:T(8,128)}, u32[]{:S(2)}) copy-start(f32[5,25]{1,0:T(8,128)} %param.5) | copy-start | bytes 1504
  11.2 39.8 %collective-permute-start.3 = (f32[137,8,384]{2,1,0:T(8,128)S(1)}, f32[137,8,384]{2,1,0:T(8,128)S(1)}, u32[]{:S(2)}, u32[]{:S(2)}) collective-permute-start(f32[137,8,384]{2,1,0:T(8,128)S(1)} %copy.20), channel_id=1, source_target_pairs={{0,2},{2,0},{1,3},{3,1},{4,6},{6,4},{5,7},{7,5},{8,10},{10,8},{9,1... | collective-permute-start | bytes 5050376 | tf_op jit(solution)/shard_map/ppermute | solution.py:18
  19.5 31.5 %copy-start.2 = (bf16[137,8,384]{2,1,0:T(8,128)(2,1)S(1)}, bf16[137,8,384]{2,1,0:T(8,128)(2,1)}, u32[]{:S(2)}) copy-start(bf16[137,8,384]{2,1,0:T(8,128)(2,1)} %param.4) | copy-start | bytes 2525188
  51.6 9.7 %collective-permute-start.4 = (bf16[137,2,384]{2,0,1:T(8,128)(2,1)S(1)}, bf16[137,2,384]{2,0,1:T(8,128)(2,1)S(1)}, u32[]{:S(2)}, u32[]{:S(2)}) collective-permute-start(bf16[137,2,384]{2,0,1:T(8,128)(2,1)S(1)} %get-tuple-element.38), channel_id=1, source_target_pairs={{0,1},{1,2},{2,3},{3,4},{4,5},{5,6},{6,7},{7,8},{8,9},{9,10},{10,1... | collective-permute-start | bytes 631304 | tf_op jit(solution)/shard_map/ppermute | solution.py:28
  51.6 9.7 %collective-permute-start.5 = (bf16[137,2,384]{2,0,1:T(8,128)(2,1)S(1)}, bf16[137,2,384]{2,0,1:T(8,128)(2,1)S(1)}, u32[]{:S(2)}, u32[]{:S(2)}) collective-permute-start(bf16[137,2,384]{2,0,1:T(8,128)(2,1)S(1)} %get-tuple-element.39), channel_id=1, source_target_pairs={{1,0},{2,1},{3,2},{4,3},{5,4},{6,5},{7,6},{8,7},{9,8},{10,9},{11,1... | collective-permute-start | bytes 631304 | tf_op jit(solution)/shard_map/ppermute | solution.py:30
  56.1 29.1 %collective-permute-start.1 = (bf16[137,2,384]{2,0,1:T(8,128)(2,1)S(1)}, bf16[137,2,384]{2,0,1:T(8,128)(2,1)S(1)}, u32[]{:S(2)}, u32[]{:S(2)}) collective-permute-start(bf16[137,2,384]{2,0,1:T(8,128)(2,1)S(1)} %get-tuple-element.40), channel_id=1, source_target_pairs={{0,1},{1,2},{2,3},{3,4},{4,5},{5,6},{6,7},{7,8},{8,9},{9,10},{10,1... | collective-permute-start | bytes 631304 | tf_op jit(solution)/shard_map/ppermute | solution.py:28
  56.2 29.0 %collective-permute-start.2 = (bf16[137,2,384]{2,0,1:T(8,128)(2,1)S(1)}, bf16[137,2,384]{2,0,1:T(8,128)(2,1)S(1)}, u32[]{:S(2)}, u32[]{:S(2)}) collective-permute-start(bf16[137,2,384]{2,0,1:T(8,128)(2,1)S(1)} %get-tuple-element.41), channel_id=1, source_target_pairs={{1,0},{2,1},{3,2},{4,3},{5,4},{6,5},{7,6},{8,7},{9,8},{10,9},{11,1... | collective-permute-start | bytes 631304 | tf_op jit(solution)/shard_map/ppermute | solution.py:30
  61.2 48.0 %collective-permute-start.6 = (f32[137,8,384]{2,1,0:T(8,128)S(1)}, f32[137,8,384]{2,1,0:T(8,128)S(1)}, u32[]{:S(2)}, u32[]{:S(2)}) collective-permute-start(f32[137,8,384]{2,1,0:T(8,128)S(1)} %copy.23), channel_id=1, source_target_pairs={{0,4},{4,0},{1,5},{5,1},{2,6},{6,2},{3,7},{7,3},{8,12},{12,8},{9,1... | collective-permute-start | bytes 5050376 | tf_op jit(solution)/shard_map/ppermute | solution.py:18
  109.7 8.6 %collective-permute-start.7 = (bf16[137,2,384]{2,0,1:T(8,128)(2,1)S(1)}, bf16[137,2,384]{2,0,1:T(8,128)(2,1)S(1)}, u32[]{:S(2)}, u32[]{:S(2)}) collective-permute-start(bf16[137,2,384]{2,0,1:T(8,128)(2,1)S(1)} %get-tuple-element.36), channel_id=1, source_target_pairs={{0,1},{1,2},{2,3},{3,4},{4,5},{5,6},{6,7},{7,8},{8,9},{9,10},{10,1... | collective-permute-start | bytes 631304 | tf_op jit(solution)/shard_map/ppermute | solution.py:28
  109.9 10.4 %collective-permute-start.8 = (bf16[137,2,384]{2,0,1:T(8,128)(2,1)S(1)}, bf16[137,2,384]{2,0,1:T(8,128)(2,1)S(1)}, u32[]{:S(2)}, u32[]{:S(2)}) collective-permute-start(bf16[137,2,384]{2,0,1:T(8,128)(2,1)S(1)} %get-tuple-element.37), channel_id=1, source_target_pairs={{1,0},{2,1},{3,2},{4,3},{5,4},{6,5},{7,6},{8,7},{9,8},{10,9},{11,1... | collective-permute-start | bytes 631304 | tf_op jit(solution)/shard_map/ppermute | solution.py:30
  115.4 74.6 %collective-permute-start.9 = (f32[137,8,384]{2,1,0:T(8,128)S(1)}, f32[137,8,384]{2,1,0:T(8,128)S(1)}, u32[]{:S(2)}, u32[]{:S(2)}) collective-permute-start(f32[137,8,384]{2,1,0:T(8,128)S(1)} %copy.26), channel_id=1, source_target_pairs={{0,8},{8,0},{1,9},{9,1},{2,10},{10,2},{3,11},{11,3},{4,12},{12,4},... | collective-permute-start | bytes 5050376 | tf_op jit(solution)/shard_map/ppermute | solution.py:18
  190.5 9.0 %collective-permute-start.10 = (bf16[137,2,384]{2,0,1:T(8,128)(2,1)S(1)}, bf16[137,2,384]{2,0,1:T(8,128)(2,1)S(1)}, u32[]{:S(2)}, u32[]{:S(2)}) collective-permute-start(bf16[137,2,384]{2,0,1:T(8,128)(2,1)S(1)} %get-tuple-element.34), channel_id=1, source_target_pairs={{0,1},{1,2},{2,3},{3,4},{4,5},{5,6},{6,7},{7,8},{8,9},{9,10},{10,1... | collective-permute-start | bytes 631304 | tf_op jit(solution)/shard_map/ppermute | solution.py:28
  190.6 9.0 %collective-permute-start.11 = (bf16[137,2,384]{2,0,1:T(8,128)(2,1)S(1)}, bf16[137,2,384]{2,0,1:T(8,128)(2,1)S(1)}, u32[]{:S(2)}, u32[]{:S(2)}) collective-permute-start(bf16[137,2,384]{2,0,1:T(8,128)(2,1)S(1)} %get-tuple-element.35), channel_id=1, source_target_pairs={{1,0},{2,1},{3,2},{4,3},{5,4},{6,5},{7,6},{8,7},{9,8},{10,9},{11,1... | collective-permute-start | bytes 631304 | tf_op jit(solution)/shard_map/ppermute | solution.py:30
  195.0 28.5 %collective-permute-start.12 = (bf16[137,2,384]{2,0,1:T(8,128)(2,1)S(1)}, bf16[137,2,384]{2,0,1:T(8,128)(2,1)S(1)}, u32[]{:S(2)}, u32[]{:S(2)}) collective-permute-start(bf16[137,2,384]{2,0,1:T(8,128)(2,1)S(1)} %get-tuple-element.32), channel_id=1, source_target_pairs={{0,1},{1,2},{2,3},{3,4},{4,5},{5,6},{6,7},{7,8},{8,9},{9,10},{10,1... | collective-permute-start | bytes 631304 | tf_op jit(solution)/shard_map/ppermute | solution.py:28
  195.1 28.5 %collective-permute-start.13 = (bf16[137,2,384]{2,0,1:T(8,128)(2,1)S(1)}, bf16[137,2,384]{2,0,1:T(8,128)(2,1)S(1)}, u32[]{:S(2)}, u32[]{:S(2)}) collective-permute-start(bf16[137,2,384]{2,0,1:T(8,128)(2,1)S(1)} %get-tuple-element.33), channel_id=1, source_target_pairs={{1,0},{2,1},{3,2},{4,3},{5,4},{6,5},{7,6},{8,7},{9,8},{10,9},{11,1... | collective-permute-start | bytes 631304 | tf_op jit(solution)/shard_map/ppermute | solution.py:30
where the time goes:
time: 251 us; the launch traced here: 249 us
  other arithmetic  120 us (48%)
  waiting for transfers between devices  80.2 us (32%)
  starting transfers between devices  26.4 us (11%)
  local copies, waits for them, and re-layouts  13 us (5%)
  between operations  6.11 us (2%)
  matrix products  3.29 us (1%)
    convert_element_type x5, other arithmetic, filter_padded(): return summed.astype(jnp.bfloat16)  111 us
    ppermute x4, waiting for transfers between devices, from_partner(): return lax.ppermute(block, axis, route)  75.2 us
    ppermute x5, starting transfers between devices, padded_2(): lax.ppermute(head, axis, [((i + 1) % count, i) for i in range(count)])  22.4 us
    slice x7, local copies, waits for them, and re-layouts, filter_padded(): weights[row_shift * 5 + col_shift] * window.astype(jnp.float32)  6.41 us
    concatenate x5, other arithmetic, padded_2(): jnp.concatenate([lax.ppermute(tail, axis, [(i, (i + 1) % count) for i in...  5.28 us
  transfers between devices with their start and end apart: 14, of which 5 were waited for; matrix products, arithmetic and copies ran while one was open for 43% of the time, Pallas kernels for 0%

commit v1 on v0

v1 whole, which is shorter than its diff:
```python
import functools

import jax
import jax.numpy as jnp
from jax import lax
from jax.experimental import pallas as pl
from jax.experimental.pallas import tpu as pltpu
from jax.sharding import PartitionSpec as P

LEVELS = 4
BANDS = 5
LANES = 128
F32 = jnp.float32
BF16 = jnp.bfloat16


def up(value, unit):
    return -(-value // unit) * unit


def swap(field, bit, count):
    return lax.ppermute(field, "lon", [(t, t ^ (1 << bit)) for t in range(count)])


def outer_swap(edge, level, count):
    route = []
    for t in range(1, count, 2):
        if (t + 1) % (2 << level) == 0:
            route += [(t, (t + 1) % count), ((t + 1) % count, t)]
    return lax.ppermute(edge, "lon", route)


def prep_kernel(taps, weights):
    row = lax.broadcasted_iota(jnp.int32, (LANES, LANES), 0)
    col = lax.broadcasted_iota(jnp.int32, (LANES, LANES), 1)
    place = (row + 2) & (LANES - 1)
    own = place >> 2
    end = place & 3
    edge_at = jnp.where(end < 2, end - 2, LANES - 2 + end)
    zero = jnp.zeros((LANES, LANES), F32)
    for k in range(BANDS):
        inside, edges = [], []
        for a in range(5):
            body, side = zero, zero
            for b in range(5):
                tap = taps[k, 5 * a + b]
                body = body + jnp.where(row - col == b - 2, tap, 0.0)
                side = side + jnp.where(edge_at - col == b - 2, tap, 0.0)
            inside.append(body.astype(BF16))
            edges.append(side)
        for u in range(6):
            for v in range(2):
                a = u - v
                block = inside[a] if 0 <= a < 5 else zero.astype(BF16)
                weights[k, u * LANES:(u + 1) * LANES, v * LANES:(v + 1) * LANES] = block
        for v in range(2):
            total = zero
            for a in range(5):
                total = total + jnp.where(own - v == a, edges[a], 0.0)
            weights[k, 6 * LANES:7 * LANES, v * LANES:(v + 1) * LANES] = total.astype(BF16)


def band_kernel(k, lons, blocks, halos, last, *refs):
    info = refs[0]
    count_r = min(k, LEVELS - 1) + 1
    refs = refs[1:]
    s0, refs = refs[0], refs[1:]
    r, refs = refs[:count_r], refs[count_r:]
    if k + 1 <= LEVELS - 1:
        r_next, refs = refs[0], refs[1:]
    else:
        r_next = None
    h, refs = dict(zip(halos, refs[:len(halos)])), refs[len(halos):]
    weights, cov, refs = refs[0], refs[1], refs[2:]
    if k > 0:
        acc_in, refs = refs[0], refs[1:]
    out, bands, ends = refs
    rows = s0.shape[1]
    pairs = lons // 2

    odd = info[0]
    far = info[1]
    outer_from = jnp.where(odd == 1, 0, lons - 2)
    inner_from = jnp.where(odd == 1, lons - 2, 0)
    outer_to = jnp.where(odd == 1, pairs + 1, 0)
    inner_to = jnp.where(odd == 1, 0, pairs + 1)

    def field(ref, at):
        return ref[pl.ds(at, 2)].astype(F32)

    def smooth(at, level):
        value = field(s0, at)
        for j in range(level):
            value = 0.5 * (value + field(r[j], at))
        return value

    def put(to, value):
        value = value.astype(BF16)
        for block in range(blocks):
            for half in range(2):
                bands[block, to, :, half * LANES:(half + 1) * LANES] = (
                    value[half, :, block * LANES:(block + 1) * LANES])

    def own(at):
        value = smooth(at, k)
        if k < LEVELS:
            value = 0.5 * (value - field(r[k], at))
        return value

    for pair in range(pairs):
        put(pair + 1, own(2 * pair))
    inner = own(inner_from)
    put(inner_to, -inner if k == 0 else inner)

    def beyond(level):
        value = smooth(outer_from, level)
        if level < LEVELS:
            partner = r[level] if level < count_r else r_next
            value = jnp.where(far == level, field(partner, outer_from), value)
        if level in h:
            first = level if level < LEVELS else level - 1
            value = jnp.where(far > first, h[level][...].astype(F32), value)
        return value

    value = beyond(k)
    if k < LEVELS:
        value = value - beyond(k + 1)
    put(outer_to, value)

    lane = lax.broadcasted_iota(jnp.int32, (rows, LANES), 1)
    none = jnp.zeros((rows, LANES), BF16)
    for block in range(blocks):
        total = none
        for n in range(lons + 4):
            at = slice((n % 2) * LANES, (n % 2 + 1) * LANES)
            after = bands[block + 1, n // 2, :, at] if block + 1 < blocks else none
            before = bands[block - 1, n // 2, :, at] if block > 0 else none
            both = jnp.where(lane < LANES // 2, after, before)
            turned = pltpu.roll(both, 4 * n, 1) if n else both
            place = (lane + 2) & (LANES - 1)
            total = jnp.where((place >> 2) == n, turned, total)
        for pair in range(pairs):
            ends[block, pair] = pltpu.roll(total, LANES - 8 * pair, 1) if pair else total

    for block in range(blocks):
        left = jnp.concatenate(
            [bands[block, 0:pairs], bands[block, 1:pairs + 1], bands[block, 2:pairs + 2], ends[block]],
            axis=2).reshape(pairs * rows, 7 * LANES)
        filtered = jnp.dot(left, weights[k], preferred_element_type=F32).astype(BF16)
        filtered = filtered.reshape(pairs, rows, 2 * LANES)
        for pair in range(pairs):
            done = jnp.dot(cov[k, block], filtered[pair], preferred_element_type=F32)
            at = slice(pair * 2 * LANES, (pair + 1) * 2 * LANES)
            if k > 0:
                done = done + acc_in[block, :, at]
            if last:
                done = done.astype(BF16)
                for half in range(2):
                    out[2 * pair + half, :, block * LANES:(block + 1) * LANES] = (
                        done[:, half * LANES:(half + 1) * LANES])
            else:
                out[block, :, at] = done


def apply_band(k, info, s0, r, h, weights, cov, acc, last):
    lons, rows, lat = s0.shape
    blocks = lat // LANES
    pairs = lons // 2
    count_r = min(k, LEVELS - 1) + 1
    halos = [level for level in (k, k + 1) if level in h]
    operands = [info, s0] + list(r[:count_r])
    if k + 1 <= LEVELS - 1:
        operands.append(r[k + 1])
    operands += [h[level] for level in halos] + [weights, cov]
    if k > 0:
        operands.append(acc)
    shape = (jax.ShapeDtypeStruct((lons, rows, lat), BF16) if last
             else jax.ShapeDtypeStruct((blocks, rows, lons * LANES), F32))
    vmem = pl.BlockSpec(memory_space=pltpu.VMEM)
    return pl.pallas_call(
        functools.partial(band_kernel, k, lons, blocks, halos, last),
        out_shape=shape,
        in_specs=[pl.BlockSpec(memory_space=pltpu.SMEM)] + [vmem] * (len(operands) - 1),
        out_specs=vmem,
        scratch_shapes=[
            pltpu.VMEM((blocks, pairs + 2, rows, 2 * LANES), BF16),
            pltpu.VMEM((blocks, pairs, rows, LANES), BF16),
        ],
        compiler_params=pltpu.CompilerParams(vmem_limit_bytes=32 << 20),
        cost_estimate=pl.CostEstimate(flops=2_000_000_000, bytes_accessed=4_000_000, transcendentals=0),
        name=f"band{k}",
    )(*operands)


def on_device(count, increment, kernels, covariance, region):
    levels, lons, lat = increment.shape
    blocks = lat // LANES
    rows = up(levels, 16)
    half, quarter = lons // 2, lons // 4
    tile = lax.axis_index("lon")
    odd = tile & 1
    second = (tile >> 1) & 1
    border = tile + odd
    far = jnp.int32(0)
    for level in range(1, count.bit_length() - 1):
        far = jnp.where(border % (1 << level) == 0, level, far)
    info = jnp.stack([odd, far]).astype(jnp.int32)
    own_region = lax.dynamic_index_in_dim(region, tile, 0, keepdims=False)

    s0 = jnp.pad(jnp.transpose(increment, (1, 0, 2)), ((0, 0), (0, rows - levels), (0, 0)))
    edge_from = odd * (lons - 2)

    r0 = swap(s0, 0, count)
    h = {0: outer_swap(lax.dynamic_slice_in_dim(s0, edge_from, 2, 0), 0, count)}

    def edge_of_half(part):
        return lax.dynamic_slice_in_dim(part, odd * (half - 2), 2, 0)

    def both(part, bit, which):
        other = swap(part, bit, count)
        low = jnp.where(which == 0, part, other)
        high = jnp.where(which == 0, other, part)
        return jnp.concatenate([low, high], 0)

    own_half = lambda x: lax.dynamic_slice_in_dim(x, odd * half, half, 0).astype(F32)
    s1 = 0.5 * (own_half(s0) + own_half(r0))
    s1_send = s1.astype(BF16)
    r1 = swap(s1_send, 1, count)
    h[1] = outer_swap(edge_of_half(s1_send), 1, count)
    s2 = 0.5 * (s1 + r1.astype(F32))
    s2_send = s2.astype(BF16)
    r2 = swap(s2_send, 2, count)
    h[2] = outer_swap(edge_of_half(s2_send), 2, count)
    s3 = 0.5 * (s2 + r2.astype(F32))
    s3_send = s3.astype(BF16)
    r3 = swap(lax.dynamic_slice_in_dim(s3_send, second * quarter, quarter, 0), 3, count)
    r1 = both(r1, 0, odd)
    r2 = both(r2, 0, odd)
    r3 = both(both(r3, 1, second), 0, odd)
    if count > 1 << LEVELS:
        h[3] = outer_swap(edge_of_half(s3_send), 3, count)
        s4 = 0.5 * (edge_of_half(s3) + edge_of_half(own_half(r3)))
        h[4] = outer_swap(s4.astype(BF16), 3, count)

    cov = jnp.stack([lax.dynamic_index_in_dim(covariance, own_region[b], 1, keepdims=False)
                     for b in range(blocks)], 1)
    cov = jnp.pad(cov, ((0, 0), (0, 0), (0, rows - levels), (0, rows - levels)))
    weights = pl.pallas_call(
        prep_kernel,
        out_shape=jax.ShapeDtypeStruct((BANDS, 7 * LANES, 2 * LANES), BF16),
        in_specs=[pl.BlockSpec(memory_space=pltpu.SMEM)],
        out_specs=pl.BlockSpec(memory_space=pltpu.VMEM),
        name="taps",
    )(kernels)

    r = [r0, r1, r2, r3]
    acc = None
    for k in range(BANDS):
        acc = apply_band(k, info, s0, r, h, weights, cov, acc, k == BANDS - 1)
    return jnp.transpose(acc[:, :levels], (1, 0, 2))


def solution(mesh):
    placed = (P(None, ("member", "lon"), None), P(), P(), P())
    return jax.shard_map(
        functools.partial(on_device, mesh.shape["lon"]),
        mesh=mesh,
        in_specs=placed,
        out_specs=P(None, ("member", "lon"), None),
        check_vma=False,
    )
```

time: 251 us -> 77.3 us (0.31)
  other arithmetic: 120 us -> 5.44 us
  waiting for transfers between devices: 80.2 us -> 13.4 us
  Pallas kernels: 0 us -> 21.8 us
  starting transfers between devices: 26.4 us -> 18.4 us
  matrix products: 3.29 us -> 0 us
    convert_element_type x9 -> x3, other arithmetic: 113 us -> 3.34 us  [the longest x1 1.3 us: on_device(): s2_send = s2.astype(BF16)]
    ppermute x14 -> x11, waiting for transfers between devices: 80.2 us -> 13.4 us  [the longest x8 13.4 us: swap(): return lax.ppermute(field, 'lon', [(t, t ^ 1 << bit) for t in range(count)])]
    pallas_call x0 -> x6, Pallas kernels: none -> 21.8 us  [the longest x5 17.9 us: apply_band(): pl.pallas_call(functools.partial(band_kernel, k, lons, blocks, halos, las...]
    ppermute x14 -> x11, starting transfers between devices: 26.4 us -> 18.4 us  [the longest x3 11.5 us: outer_swap(): return lax.ppermute(edge, 'lon', route)]
    slice x14 -> x1, local copies, waits for them, and re-layouts: 7.71 us -> 0.59 us  [on_device(): own_region[b]]
    dynamic_slice x6 -> x5, local copies, waits for them, and re-layouts: 2.31 us -> 8.37 us  [the longest x1 5.66 us: on_device(): lax.dynamic_index_in_dim(covariance, own_region[b], 1, keepdims=False)]
    concatenate x5 -> x4, other arithmetic: 5.28 us -> 0.36 us  [both(): return jnp.concatenate([low, high], 0)]
    dot_general x15 -> x0, matrix products: 3.29 us -> none  [apply_blocks(): jnp.einsum('ab,bxr->axr', matrix, columns, preferred_element_type=jnp.flo...]
  transfers between devices with their start and end apart: 14 -> 11, of which waited for: 5 -> 3; matrix products, arithmetic and copies ran while one was open for 43% -> 18% of each run, Pallas kernels for 0% -> 14%
where the time goes in v1:
time: 77.3 us; the launch traced here: 76.7 us
  Pallas kernels  21.8 us (28%)
  starting transfers between devices  18.4 us (24%)
  waiting for transfers between devices  13.4 us (17%)
  local copies, waits for them, and re-layouts  11.7 us (15%)
  between operations  5.92 us (8%)
  other arithmetic  5.44 us (7%)
    pallas_call x5, Pallas kernels, apply_band(): pl.pallas_call(functools.partial(band_kernel, k, lons, blocks, halos, las...  17.9 us
    ppermute x8, waiting for transfers between devices, swap(): return lax.ppermute(field, 'lon', [(t, t ^ 1 << bit) for t in range(count)])  13.4 us
    ppermute x3, starting transfers between devices, outer_swap(): return lax.ppermute(edge, 'lon', route)  11.5 us
    ppermute x8, starting transfers between devices, swap(): return lax.ppermute(field, 'lon', [(t, t ^ 1 << bit) for t in range(count)])  6.9 us
    dynamic_slice x1, local copies, waits for them, and re-layouts, on_device(): lax.dynamic_index_in_dim(covariance, own_region[b], 1, keepdims=False)  5.66 us
    pallas_call x1, Pallas kernels, on_device(): pl.pallas_call(prep_kernel, out_shape=jax.ShapeDtypeStruct((BANDS, 7 * LA...  3.93 us
    dynamic_slice x2, local copies, waits for them, and re-layouts, edge_of_half(): return lax.dynamic_slice_in_dim(part, odd * (half - 2), 2, 0)  1.92 us
  transfers between devices with their start and end apart: 11, of which 3 were waited for; matrix products, arithmetic and copies ran while one was open for 18% of the time, Pallas kernels for 14%

profile of v1, /device:TPU:0, one launch (start us, length us, event | category | flops | bytes accessed | tf_op | source)
XLA Modules:
  0.0 76.7 jit_solution(411386686659713258)
XLA Ops:
  0.0 1.3 %copy.14 = bf16[137,8,384]{2,0,1:T(8,128)(2,1)S(1)} copy(bf16[137,8,384]{2,1,0:T(8,128)(2,1)} %param.4) | data formatting | bytes 1683456 | tf_op args[0]
  1.9 2.1 %collective-permute-done.refs_2_ = bf16[8,144,384]{2,1,0:T(8,128)(2,1)S(1)} collective-permute-done((bf16[8,144,384]{2,1,0:T(8,128)(2,1)S(1)}, bf16[8,144,384]{2,1,0:T(8,128)(2,1)S(1)}, u32[]{:S(2)}, u32[]{:S(2)}) %collective-permute-start) | collective-permute-done | bytes 884768 | tf_op jit(solution)/shard_map/ppermute | solution.py:22
  4.0 0.9 %fusion.9 = bf16[4,144,384]{2,1,0:T(8,128)(2,1)} fusion(bf16[8,144,384]{2,1,0:T(8,128)(2,1)S(1)} %collective-permute-done.refs_2_, s32[]{:T(128)S(6)} %select_n.100, bf16[8,137,384]{2,1,0:T(8,128)(2,1)S(1)} %bitcast.11), kind=kLoop, calls=%fused_computation.18 | loop fusion | flops 1105920 | bytes 1726468 | tf_op jit(solution)/shard_map/convert_element_type | solution.py:227
  4.9 2.9 %collective-permute-start.1 = (bf16[4,144,384]{2,1,0:T(8,128)(2,1)}, bf16[4,144,384]{2,1,0:T(8,128)(2,1)S(1)}, u32[]{:S(2)}, u32[]{:S(2)}) collective-permute-start(bf16[4,144,384]{2,1,0:T(8,128)(2,1)} %fusion.9), channel_id=1, source_target_pairs={{0,2},{1,3},{2,0},{3,1},{4,6},{5,7},{6,4},{7,5},{8,10},{9,11},{10,... | collective-permute-start | bytes 1327112 | tf_op jit(solution)/shard_map/ppermute | solution.py:22
  7.7 0.7 constant_dynamic-slice_fusion
  8.4 3.0 %collective-permute-start.10 = (bf16[2,144,384]{2,1,0:T(8,128)(2,1)}, bf16[2,144,384]{2,1,0:T(8,128)(2,1)S(1)}, u32[]{:S(2)}, u32[]{:S(2)}) collective-permute-start(bf16[2,144,384]{2,1,0:T(8,128)(2,1)} %constant_dynamic-slice_fusion), channel_id=1, source_target_pairs={{1,2},{2,1},{3,4},{4,3},{5,6},{6,5},{7,8},{8,7},{9,10},{10,9},{11,... | collective-permute-start | bytes 663560 | tf_op jit(solution)/shard_map/ppermute | solution.py:30
  17.8 5.7 %constant_dynamic-slice_fusion.5 = (bf16[5,1,137,137]{3,1,2,0:T(2,128)(2,1)S(1)}, bf16[5,1,137,137]{3,1,2,0:T(2,128)(2,1)S(1)}, bf16[5,1,137,137]{3,1,2,0:T(2,128)(2,1)S(1)}) fusion(bf16[5,16,137,137]{3,1,2,0:T(8,128)(2,1)} %param.6, s32[]{:T(128)S(6)} %select_n.112, s32[]{:T(128)S(6)} %select_n.113, s32[]{:T(128)S(6)} %select_n.114), kind=kLoop, calls=%fused_computation.36 | loop fusion | bytes 1126152 | tf_op jit(solution)/shard_map/jit(dynamic_index_in_dim)/dynamic_slice | solution.py:245
  23.7 1.3 %fusion.12 = (bf16[4,144,384]{2,1,0:T(8,128)(2,1)}, f32[4,144,384]{2,1,0:T(8,128)}) fusion(bf16[4,144,384]{2,1,0:T(8,128)(2,1)S(1)} %collective-permute-done.1, bf16[8,144,384]{2,1,0:T(8,128)(2,1)S(1)} %collective-permute-done.refs_2_, s32[]{:T(128)S(6)} %select_n.100, bf16[8,137,384]{2,1,0:T(8,128)(2,1)S(1)} %bitcast.13), kind=kLoop, calls=%fused_computation.39 | loop fusion | flops 1769472 | bytes 3053572 | tf_op jit(solution)/shard_map/convert_element_type | solution.py:231
  25.3 3.9 %taps.2.refs_6_.refs_7_ = bf16[5,896,256]{2,1,0:T(8,128)(2,1)} custom-call(f32[5,25]{1,0:T(8,128)} %taps.3), custom_call_target="tpu_custom_call" | custom-call | tf_op jit(solution)/shard_map/taps/pallas_call | solution.py:248
  29.3 1.0 %constant_dynamic-slice_fusion.1 = bf16[2,144,384]{2,1,0:T(8,128)(2,1)S(1)} fusion(bf16[4,144,384]{2,1,0:T(8,128)(2,1)} %fusion.9, s32[]{:T(128)S(6)} %select_n.115), kind=kLoop, calls=%fused_computation.32 | loop fusion | bytes 442372 | tf_op jit(solution)/shard_map/dynamic_slice | solution.py:217
  30.3 5.2 %collective-permute-start.9 = (bf16[2,144,384]{2,1,0:T(8,128)(2,1)S(1)}, bf16[2,144,384]{2,1,0:T(8,128)(2,1)S(1)}, u32[]{:S(2)}, u32[]{:S(2)}) collective-permute-start(bf16[2,144,384]{2,1,0:T(8,128)(2,1)S(1)} %constant_dynamic-slice_fusion.1), channel_id=1, source_target_pairs={{3,4},{4,3},{7,8},{8,7},{11,12},{12,11},{15,0},{0,15},{19,20},{20,... | collective-permute-start | bytes 663560 | tf_op jit(solution)/shard_map/ppermute | solution.py:30
  35.4 1.0 %constant_dynamic-slice_fusion.2 = bf16[2,144,384]{2,1,0:T(8,128)(2,1)S(1)} fusion(bf16[4,144,384]{2,1,0:T(8,128)(2,1)} %get-tuple-element.5, s32[]{:T(128)S(6)} %select_n.115), kind=kLoop, calls=%fused_computation.33 | loop fusion | bytes 442372 | tf_op jit(solution)/shard_map/dynamic_slice | solution.py:217
  36.4 3.3 %collective-permute-start.8 = (bf16[2,144,384]{2,1,0:T(8,128)(2,1)S(1)}, bf16[2,144,384]{2,1,0:T(8,128)(2,1)S(1)}, u32[]{:S(2)}, u32[]{:S(2)}) collective-permute-start(bf16[2,144,384]{2,1,0:T(8,128)(2,1)S(1)} %constant_dynamic-slice_fusion.2), channel_id=1, source_target_pairs={{7,8},{8,7},{15,0},{0,15},{23,24},{24,23},{31,16},{16,31}} | collective-permute-start | bytes 663560 | tf_op jit(solution)/shard_map/ppermute | solution.py:30
  39.7 1.1 %fusion.11 = bf16[2,144,384]{2,1,0:T(8,128)(2,1)S(1)} fusion(f32[4,144,384]{2,1,0:T(8,128)} %get-tuple-element.6, s32[]{:T(128)S(6)} %select_n.106, bf16[4,144,384]{2,1,0:T(8,128)(2,1)} %collective-permute-done.3), kind=kLoop, calls=%fused_computation.21 | loop fusion | flops 442368 | bytes 884740 | tf_op jit(solution)/shard_map/convert_element_type | solution.py:235
  41.0 9.8 %collective-permute-done.5 = bf16[2,144,384]{2,1,0:T(8,128)(2,1)S(1)} collective-permute-done((bf16[2,144,384]{2,1,0:T(8,128)(2,1)S(1)}, bf16[2,144,384]{2,1,0:T(8,128)(2,1)S(1)}, u32[]{:S(2)}, u32[]{:S(2)}) %collective-permute-start.5) | collective-permute-done | bytes 221216 | tf_op jit(solution)/shard_map/ppermute | solution.py:22
  50.9 3.3 %collective-permute-start.6 = (bf16[2,144,384]{2,1,0:T(8,128)(2,1)S(1)}, bf16[2,144,384]{2,1,0:T(8,128)(2,1)S(1)}, u32[]{:S(2)}, u32[]{:S(2)}) collective-permute-start(bf16[2,144,384]{2,1,0:T(8,128)(2,1)S(1)} %collective-permute-done.5), channel_id=1, source_target_pairs={{0,2},{1,3},{2,0},{3,1},{4,6},{5,7},{6,4},{7,5},{8,10},{9,11},{10,... | collective-permute-start | bytes 663560 | tf_op jit(solution)/shard_map/ppermute | solution.py:22
  54.4 3.1 %band0.1.refs_9_ = f32[3,144,1024]{2,1,0:T(8,128)S(1)} custom-call(s32[2]{0:T(128)S(1)} %pad_add_fusion.refs_0_, bf16[8,144,384]{2,1,0:T(8,128)(2,1)S(1)} %pad.8.refs_1_, bf16[8,144,384]{2,1,0:T(8,128)(2,1)S(1)} %collective-permute-done.refs_2_, bf16[8,144,384]{2,1,0:T(8,128)(2,1)S(1)} %pad_maximum_fusion.refs_3_, ...), custom_call_target="tpu_custom_call" | custom-call | flops 2000000000 | bytes 4000000 | tf_op jit(solution)/shard_map/band0/pallas_call | solution.py:180
  57.5 1.5 %collective-permute-done.6 = bf16[2,144,384]{2,1,0:T(8,128)(2,1)S(1)} collective-permute-done((bf16[2,144,384]{2,1,0:T(8,128)(2,1)S(1)}, bf16[2,144,384]{2,1,0:T(8,128)(2,1)S(1)}, u32[]{:S(2)}, u32[]{:S(2)}) %collective-permute-start.6) | collective-permute-done | bytes 221216 | tf_op jit(solution)/shard_map/ppermute | solution.py:22
  59.2 1.1 %broadcast_select_fusion.3 = (bf16[4,144,384]{2,1,0:T(8,128)(2,1)S(1)}, bf16[4,144,384]{2,1,0:T(8,128)(2,1)S(1)}) fusion(bf16[4,144,384]{2,1,0:T(8,128)(2,1)} %collective-permute-done.3, bf16[4,144,384]{2,1,0:T(8,128)(2,1)S(1)} %collective-permute-done.4, pred[]{:T(512)S(6)} %eq.28), kind=kLoop, calls=%fused_computation.26 | loop fusion | flops 442368 | bytes 1769473 | tf_op jit(solution)/shard_map/jit(_where)/select_n | solution.py:221
  60.4 3.4 %band1.1.refs_9_ = f32[3,144,1024]{2,1,0:T(8,128)S(1)} custom-call(s32[2]{0:T(128)S(1)} %pad_add_fusion.refs_0_, bf16[8,144,384]{2,1,0:T(8,128)(2,1)S(1)} %pad.8.refs_1_, bf16[8,144,384]{2,1,0:T(8,128)(2,1)S(1)} %collective-permute-done.refs_2_, bf16[8,144,384]{2,1,0:T(8,128)(2,1)S(1)} %pad_maximum_fusion.refs_3_, ...), custom_call_target="tpu_custom_call" | custom-call | flops 2000000000 | bytes 4000000 | tf_op jit(solution)/shard_map/band1/pallas_call | solution.py:180
  64.1 3.7 %band2.1.refs_8_ = f32[3,144,1024]{2,1,0:T(8,128)S(1)} custom-call(s32[2]{0:T(128)S(1)} %pad_add_fusion.refs_0_, bf16[8,144,384]{2,1,0:T(8,128)(2,1)S(1)} %pad.8.refs_1_, bf16[8,144,384]{2,1,0:T(8,128)(2,1)S(1)} %collective-permute-done.refs_2_, bf16[8,144,384]{2,1,0:T(8,128)(2,1)S(1)} %pad_maximum_fusion.refs_3_, ...), custom_call_target="tpu_custom_call" | custom-call | flops 2000000000 | bytes 4000000 | tf_op jit(solution)/shard_map/band2/pallas_call | solution.py:180
  67.8 3.9 %band3.1.refs_8_ = f32[3,144,1024]{2,1,0:T(8,128)S(1)} custom-call(s32[2]{0:T(128)S(1)} %pad_add_fusion.refs_0_, bf16[8,144,384]{2,1,0:T(8,128)(2,1)S(1)} %pad.8.refs_1_, bf16[8,144,384]{2,1,0:T(8,128)(2,1)S(1)} %collective-permute-done.refs_2_, bf16[8,144,384]{2,1,0:T(8,128)(2,1)S(1)} %pad_maximum_fusion.refs_3_, ...), custom_call_target="tpu_custom_call" | custom-call | flops 2000000000 | bytes 4000000 | tf_op jit(solution)/shard_map/band3/pallas_call | solution.py:180
  71.6 3.9 %band4.1 = bf16[8,144,384]{2,1,0:T(8,128)(2,1)S(1)} custom-call(s32[2]{0:T(128)S(1)} %pad_add_fusion.refs_0_, bf16[8,144,384]{2,1,0:T(8,128)(2,1)S(1)} %pad.8.refs_1_, bf16[8,144,384]{2,1,0:T(8,128)(2,1)S(1)} %collective-permute-done.refs_2_, bf16[8,144,384]{2,1,0:T(8,128)(2,1)S(1)} %pad_maximum_fusion.refs_3_, ...), custom_call_target="tpu_custom_call" | custom-call | flops 2000000000 | bytes 4000000 | tf_op jit(solution)/shard_map/band4/pallas_call | solution.py:180
  75.6 1.1 %copy.9 = bf16[137,8,384]{2,1,0:T(8,128)(2,1)} copy(bf16[137,8,384]{2,0,1:T(8,128)(2,1)S(1)} %slice_bitcast_fusion) | data formatting | bytes 1683456 | tf_op jit(solution)/shard_map/transpose | solution.py:260
  (34 shorter events, 2.8 us)
Async XLA Ops:
  0.0 11.5 %copy-start = (s32[16,3]{0,1:T(4,128)S(1)}, s32[16,3]{0,1:T(4,128)}, u32[]{:S(2)}) copy-start(s32[16,3]{0,1:T(4,128)} %param.7) | copy-start | bytes 580
  1.4 2.6 %collective-permute-start = (bf16[8,144,384]{2,1,0:T(8,128)(2,1)S(1)}, bf16[8,144,384]{2,1,0:T(8,128)(2,1)S(1)}, u32[]{:S(2)}, u32[]{:S(2)}) collective-permute-start(bf16[8,144,384]{2,1,0:T(8,128)(2,1)S(1)} %pad.8.refs_1_), channel_id=1, source_target_pairs={{0,1},{1,0},{2,3},{3,2},{4,5},{5,4},{6,7},{7,6},{8,9},{9,8},{10,11... | collective-permute-start | bytes 2654216 | tf_op jit(solution)/shard_map/ppermute | solution.py:22
  4.9 18.8 %collective-permute-start.1 = (bf16[4,144,384]{2,1,0:T(8,128)(2,1)}, bf16[4,144,384]{2,1,0:T(8,128)(2,1)S(1)}, u32[]{:S(2)}, u32[]{:S(2)}) collective-permute-start(bf16[4,144,384]{2,1,0:T(8,128)(2,1)} %fusion.9), channel_id=1, source_target_pairs={{0,2},{1,3},{2,0},{3,1},{4,6},{5,7},{6,4},{7,5},{8,10},{9,11},{10,... | collective-permute-start | bytes 1327112 | tf_op jit(solution)/shard_map/ppermute | solution.py:22
  8.4 45.9 %collective-permute-start.10 = (bf16[2,144,384]{2,1,0:T(8,128)(2,1)}, bf16[2,144,384]{2,1,0:T(8,128)(2,1)S(1)}, u32[]{:S(2)}, u32[]{:S(2)}) collective-permute-start(bf16[2,144,384]{2,1,0:T(8,128)(2,1)} %constant_dynamic-slice_fusion), channel_id=1, source_target_pairs={{1,2},{2,1},{3,4},{4,3},{5,6},{6,5},{7,8},{8,7},{9,10},{10,9},{11,... | collective-permute-start | bytes 663560 | tf_op jit(solution)/shard_map/ppermute | solution.py:30
  25.0 14.7 %collective-permute-start.3 = (bf16[4,144,384]{2,1,0:T(8,128)(2,1)}, bf16[4,144,384]{2,1,0:T(8,128)(2,1)}, u32[]{:S(2)}, u32[]{:S(2)}) collective-permute-start(bf16[4,144,384]{2,1,0:T(8,128)(2,1)} %get-tuple-element.5), channel_id=1, source_target_pairs={{0,4},{1,5},{2,6},{3,7},{4,0},{5,1},{6,2},{7,3},{8,12},{9,13},{10,... | collective-permute-start | bytes 1327112 | tf_op jit(solution)/shard_map/ppermute | solution.py:22
  29.2 11.7 %collective-permute-start.2 = (bf16[4,144,384]{2,1,0:T(8,128)(2,1)S(1)}, bf16[4,144,384]{2,1,0:T(8,128)(2,1)S(1)}, u32[]{:S(2)}, u32[]{:S(2)}) collective-permute-start(bf16[4,144,384]{2,1,0:T(8,128)(2,1)S(1)} %collective-permute-done.1), channel_id=1, source_target_pairs={{0,1},{1,0},{2,3},{3,2},{4,5},{5,4},{6,7},{7,6},{8,9},{9,8},{10,11... | collective-permute-start | bytes 1327112 | tf_op jit(solution)/shard_map/ppermute | solution.py:22
  30.3 24.1 %collective-permute-start.9 = (bf16[2,144,384]{2,1,0:T(8,128)(2,1)S(1)}, bf16[2,144,384]{2,1,0:T(8,128)(2,1)S(1)}, u32[]{:S(2)}, u32[]{:S(2)}) collective-permute-start(bf16[2,144,384]{2,1,0:T(8,128)(2,1)S(1)} %constant_dynamic-slice_fusion.1), channel_id=1, source_target_pairs={{3,4},{4,3},{7,8},{8,7},{11,12},{12,11},{15,0},{0,15},{19,20},{20,... | collective-permute-start | bytes 663560 | tf_op jit(solution)/shard_map/ppermute | solution.py:30
  36.4 24.0 %collective-permute-start.8 = (bf16[2,144,384]{2,1,0:T(8,128)(2,1)S(1)}, bf16[2,144,384]{2,1,0:T(8,128)(2,1)S(1)}, u32[]{:S(2)}, u32[]{:S(2)}) collective-permute-start(bf16[2,144,384]{2,1,0:T(8,128)(2,1)S(1)} %constant_dynamic-slice_fusion.2), channel_id=1, source_target_pairs={{7,8},{8,7},{15,0},{0,15},{23,24},{24,23},{31,16},{16,31}} | collective-permute-start | bytes 663560 | tf_op jit(solution)/shard_map/ppermute | solution.py:30
  40.8 13.5 %copy-start.1 = (bf16[5,896,256]{2,1,0:T(8,128)(2,1)S(1)}, bf16[5,896,256]{2,1,0:T(8,128)(2,1)}, u32[]{:S(2)}) copy-start(bf16[5,896,256]{2,1,0:T(8,128)(2,1)} %taps.2.refs_6_.refs_7_) | copy-start | bytes 6881284
  40.8 10.0 %collective-permute-start.5 = (bf16[2,144,384]{2,1,0:T(8,128)(2,1)S(1)}, bf16[2,144,384]{2,1,0:T(8,128)(2,1)S(1)}, u32[]{:S(2)}, u32[]{:S(2)}) collective-permute-start(bf16[2,144,384]{2,1,0:T(8,128)(2,1)S(1)} %fusion.11), channel_id=1, source_target_pairs={{0,8},{1,9},{2,10},{3,11},{4,12},{5,13},{6,14},{7,15},{8,0},{9,1},... | collective-permute-start | bytes 663560 | tf_op jit(solution)/shard_map/ppermute | solution.py:22
  50.9 8.1 %collective-permute-start.6 = (bf16[2,144,384]{2,1,0:T(8,128)(2,1)S(1)}, bf16[2,144,384]{2,1,0:T(8,128)(2,1)S(1)}, u32[]{:S(2)}, u32[]{:S(2)}) collective-permute-start(bf16[2,144,384]{2,1,0:T(8,128)(2,1)S(1)} %collective-permute-done.5), channel_id=1, source_target_pairs={{0,2},{1,3},{2,0},{3,1},{4,6},{5,7},{6,4},{7,5},{8,10},{9,11},{10,... | collective-permute-start | bytes 663560 | tf_op jit(solution)/shard_map/ppermute | solution.py:22
  54.3 4.9 %collective-permute-start.4 = (bf16[4,144,384]{2,1,0:T(8,128)(2,1)}, bf16[4,144,384]{2,1,0:T(8,128)(2,1)S(1)}, u32[]{:S(2)}, u32[]{:S(2)}) collective-permute-start(bf16[4,144,384]{2,1,0:T(8,128)(2,1)} %collective-permute-done.3), channel_id=1, source_target_pairs={{0,1},{1,0},{2,3},{3,2},{4,5},{5,4},{6,7},{7,6},{8,9},{9,8},{10,11... | collective-permute-start | bytes 1327112 | tf_op jit(solution)/shard_map/ppermute | solution.py:22
  59.1 4.7 %collective-permute-start.7 = (bf16[4,144,384]{2,1,0:T(8,128)(2,1)S(1)}, bf16[4,144,384]{2,1,0:T(8,128)(2,1)S(1)}, u32[]{:S(2)}, u32[]{:S(2)}) collective-permute-start(bf16[4,144,384]{2,1,0:T(8,128)(2,1)S(1)} %pad_maximum_fusion.3), channel_id=1, source_target_pairs={{0,1},{1,0},{2,3},{3,2},{4,5},{5,4},{6,7},{7,6},{8,9},{9,8},{10,11... | collective-permute-start | bytes 1327112 | tf_op jit(solution)/shard_map/ppermute | solution.py:22

commit v2 on v0

v2 whole, which is shorter than its diff:
```python
import functools

import jax
import jax.numpy as jnp
from jax import lax
from jax.experimental import pallas as pl
from jax.experimental.pallas import tpu as pltpu
from jax.sharding import PartitionSpec as P

LEVELS = 4
BANDS = 5
LANES = 128
F32 = jnp.float32
BF16 = jnp.bfloat16


def up(value, unit):
    return -(-value // unit) * unit


def swap(field, bit, count):
    return lax.ppermute(field, "lon", [(t, t ^ (1 << bit)) for t in range(count)])


def outer_swap(edge, level, count, only=False):
    route = []
    for t in range(1, count, 2):
        if (t + 1) % (2 << level) == 0 and not (only and (t + 1) % (4 << level) == 0):
            route += [(t, (t + 1) % count), ((t + 1) % count, t)]
    return lax.ppermute(edge, "lon", route)


def prep_kernel(taps, weights, masks):
    row = lax.broadcasted_iota(jnp.int32, (LANES, LANES), 0)
    col = lax.broadcasted_iota(jnp.int32, (LANES, LANES), 1)
    for b in range(5):
        masks[b] = jnp.where(row - col == b - 2, 1.0, 0.0)
    own = ((row + 2) & (LANES - 1)) >> 2
    end = (lax.broadcasted_iota(jnp.int32, (8, LANES), 0) + 2) & 3
    edge_at = jnp.where(end < 2, end - 2, LANES - 2 + end)
    reach = edge_at - lax.broadcasted_iota(jnp.int32, (8, LANES), 1)
    zero = jnp.zeros((LANES, LANES), BF16)
    for k in range(BANDS):
        inside, edges = [], []
        for a in range(5):
            body = taps[k, 5 * a] * masks[0]
            side = jnp.zeros((8, LANES), F32)
            for b in range(5):
                if b:
                    body = body + taps[k, 5 * a + b] * masks[b]
                side = jnp.where(reach == b - 2, taps[k, 5 * a + b], side)
            inside.append(body.astype(BF16))
            edges.append(jnp.concatenate([side] * (LANES // 8), 0))
        for u in range(6):
            for v in range(2):
                a = u - v
                block = inside[a] if 0 <= a < 5 else zero
                weights[k, u * LANES:(u + 1) * LANES, v * LANES:(v + 1) * LANES] = block
        for v in range(2):
            total = jnp.zeros((LANES, LANES), F32)
            for a in range(5):
                total = jnp.where(own == a + v, edges[a], total)
            weights[k, 6 * LANES:7 * LANES, v * LANES:(v + 1) * LANES] = total.astype(BF16)


def filter_bands(ks, lons, blocks, info, s0, r, h, weights, bands, ends, store):
    r, next_edge = r
    rows = s0.shape[1]
    pairs = lons // 2
    odd, far = info[0], info[1]
    outer_from = jnp.where(odd == 1, 0, lons - 2)
    inner_from = jnp.where(odd == 1, lons - 2, 0)
    outer_to = jnp.where(odd == 1, pairs + 1, 0)
    inner_to = jnp.where(odd == 1, 0, pairs + 1)

    def field(ref, at):
        return ref[pl.ds(at, 2)].astype(F32)

    def smooth(at, level):
        value = field(s0, at)
        for j in range(level):
            value = 0.5 * (value + field(r[j], at))
        return value

    def put(i, to, value):
        value = value.astype(BF16)
        for block in range(blocks):
            for half in range(2):
                bands[i, block, to, :, half * LANES:(half + 1) * LANES] = (
                    value[half, :, block * LANES:(block + 1) * LANES])

    def own(at):
        value = smooth(at, ks[0])
        got = []
        for k in ks:
            if k < LEVELS:
                partner = field(r[k], at)
                got.append(0.5 * (value - partner))
                value = 0.5 * (value + partner)
            else:
                got.append(value)
        return got

    for pair in range(pairs):
        for i, value in enumerate(own(2 * pair)):
            put(i, pair + 1, value)
    for i, value in enumerate(own(inner_from)):
        put(i, inner_to, -value if ks[i] == 0 else value)

    beyond = {}
    value = smooth(outer_from, ks[0])
    for level in range(ks[0], min(ks[-1] + 1, LEVELS) + 1):
        at_border = value
        if level < LEVELS:
            partner = field(r[level], outer_from) if level < len(r) else next_edge[...].astype(F32)
            at_border = jnp.where(far == level, partner, value)
            value = 0.5 * (value + partner)
        if level in h:
            first = level if level < LEVELS else level - 1
            at_border = jnp.where(far > first, h[level][...].astype(F32), at_border)
        beyond[level] = at_border
    for i, k in enumerate(ks):
        put(i, outer_to, beyond[k] - beyond[k + 1] if k < LEVELS else beyond[k])

    lane = lax.broadcasted_iota(jnp.int32, (rows, LANES), 1)
    place = ((lane + 2) & (LANES - 1)) >> 2
    none = jnp.zeros((rows, LANES), BF16)
    for i, k in enumerate(ks):
        for block in range(blocks):
            total = none
            for n in range(lons + 4):
                at = slice((n % 2) * LANES, (n % 2 + 1) * LANES)
                after = bands[i, block + 1, n // 2, :, at] if block + 1 < blocks else none
                before = bands[i, block - 1, n // 2, :, at] if block > 0 else none
                both = jnp.where(lane < LANES // 2, after, before)
                turned = pltpu.roll(both, 4 * n, 1) if n else both
                total = jnp.where(place == n, turned, total)
            for pair in range(pairs):
                ends[block, pair] = pltpu.roll(total, LANES - 8 * pair, 1) if pair else total
        for block in range(blocks):
            left = jnp.concatenate(
                [bands[i, block, 0:pairs], bands[i, block, 1:pairs + 1],
                 bands[i, block, 2:pairs + 2], ends[block]],
                axis=2).reshape(pairs * rows, 7 * LANES)
            filtered = jnp.dot(left, weights[k], preferred_element_type=F32).astype(BF16)
            store(i, block, filtered.reshape(pairs, rows, 2 * LANES))


def split_refs(refs, ks, halos):
    info, s0, refs = refs[0], refs[1], refs[2:]
    count_r = min(ks[-1] + 1, LEVELS)
    r, refs = refs[:count_r], refs[count_r:]
    next_edge = None
    if count_r < LEVELS:
        next_edge, refs = refs[0], refs[1:]
    h, refs = dict(zip(halos, refs[:len(halos)])), refs[len(halos):]
    return info, s0, (r, next_edge), h, refs[0], refs[1:]


def filter_kernel(ks, lons, blocks, halos, *refs):
    info, s0, r, h, weights, refs = split_refs(refs, ks, halos)
    out, bands, ends = refs

    def store(i, block, value):
        out[i, block] = value

    filter_bands(ks, lons, blocks, info, s0, r, h, weights, bands, ends, store)


def last_kernel(ks, lons, blocks, halos, *refs):
    info, s0, r, h, weights, refs = split_refs(refs, ks, halos)
    cov, acc, out, bands, ends, done = refs
    rows = s0.shape[1]
    pairs = lons // 2

    def store(i, block, value):
        done[i, block] = value

    filter_bands(ks, lons, blocks, info, s0, r, h, weights, bands, ends, store)
    for block in range(blocks):
        for pair in range(pairs):
            at = slice(pair * 2 * LANES, (pair + 1) * 2 * LANES)
            total = acc[block, :, at]
            for i, k in enumerate(ks):
                total = total + jnp.dot(cov[k, block, :, :rows], done[i, block, pair], preferred_element_type=F32)
            total = total.astype(BF16)
            for half in range(2):
                out[2 * pair + half, :, block * LANES:(block + 1) * LANES] = (
                    total[:, half * LANES:(half + 1) * LANES])


def vertical_kernel(lons, blocks, cov, *refs):
    parts, out = refs[:-1], refs[-1]
    rows = out.shape[1]
    for block in range(blocks):
        for pair in range(lons // 2):
            total, k = None, 0
            for part in parts:
                for i in range(part.shape[0]):
                    more = jnp.dot(cov[k, block, :, :rows], part[i, block, pair], preferred_element_type=F32)
                    total = more if total is None else total + more
                    k += 1
            out[block, :, pair * 2 * LANES:(pair + 1) * 2 * LANES] = total


def choose_kernel(levels, rows, blocks, place, region, every, chosen, wide, tail):
    regions = every.shape[2]
    tile = place[2]
    wide[levels * regions:, :] = jnp.zeros((wide.shape[0] - levels * regions, LANES), F32)
    tail[...] = jnp.zeros(tail.shape, F32)
    for k in range(BANDS):
        flat = every[k].astype(F32).reshape(levels * regions, levels)
        wide[:levels * regions, :] = flat[:, :LANES]
        tail[:levels * regions, :levels - LANES] = flat[:, LANES:]
        for block in range(blocks):
            at = pl.ds(region[tile, block], rows, stride=regions)
            chosen[k, block, :, :LANES] = wide[at, :].astype(BF16)
            chosen[k, block, :, LANES:] = tail[at, :].astype(BF16)


VMEM = pl.BlockSpec(memory_space=pltpu.VMEM)
SMEM = pl.BlockSpec(memory_space=pltpu.SMEM)


def cost(flops, data):
    return pl.CostEstimate(flops=int(flops), bytes_accessed=int(data), transcendentals=0)


def filter_part(ks, info, s0, r, h, weights, name, flops, cov=None, acc=None):
    lons, rows, lat = s0.shape
    blocks, pairs = lat // LANES, lons // 2
    halos = [level for level in range(ks[0], min(ks[-1] + 1, LEVELS) + 1) if level in h]
    operands = [info, s0, *r, *[h[level] for level in halos], weights]
    scratch = [pltpu.VMEM((len(ks), blocks, pairs + 2, rows, 2 * LANES), BF16),
               pltpu.VMEM((blocks, pairs, rows, LANES), BF16)]
    if cov is None:
        kernel = filter_kernel
        shape = jax.ShapeDtypeStruct((len(ks), blocks, pairs, rows, 2 * LANES), BF16)
    else:
        kernel = last_kernel
        operands += [cov, acc]
        scratch.append(pltpu.VMEM((len(ks), blocks, pairs, rows, 2 * LANES), BF16))
        shape = jax.ShapeDtypeStruct((lons, rows, lat), BF16)
    return pl.pallas_call(
        functools.partial(kernel, ks, lons, blocks, halos),
        out_shape=shape,
        in_specs=[SMEM] + [VMEM] * (len(operands) - 1),
        out_specs=VMEM,
        scratch_shapes=scratch,
        compiler_params=pltpu.CompilerParams(vmem_limit_bytes=14 << 20),
        cost_estimate=cost(flops, 1e6),
        name=name,
    )(*operands)


def on_device(count, increment, kernels, covariance, region):
    levels, lons, lat = increment.shape
    blocks = lat // LANES
    rows = up(levels, 16)
    tile = lax.axis_index("lon")
    odd = tile & 1
    second = (tile >> 1) & 1
    border = tile + odd
    far = jnp.int32(0)
    for level in range(1, count.bit_length() - 1):
        far = jnp.where(border % (1 << level) == 0, level, far)
    info = jnp.stack([odd, far, tile]).astype(jnp.int32)

    def on_rows(x):
        return jnp.pad(jnp.transpose(x, (1, 0, 2)), ((0, 0), (0, rows - levels), (0, 0)))

    def pick(which, x):
        middle = x.shape[0] // 2
        return jnp.where(which == 1, x[:middle], x[middle:])

    def pair_up(which, mine, other):
        return jnp.concatenate([jnp.where(which == 1, mine, other), jnp.where(which == 1, other, mine)], 0)

    def edge(x):
        return jnp.where(odd == 1, x[-2:], x[:2])

    def far_edge(x):
        return jnp.where(odd == 1, x[:2], x[-2:])

    def mean(a, b):
        return 0.5 * (a.astype(F32) + b.astype(F32))

    def after(x, y):
        return lax.optimization_barrier((x, y))

    def gather(x, bit, which):
        return pair_up(which, x, swap(x, bit, count))

    partner = swap(increment, 0, count)
    s0 = on_rows(increment)
    r0 = on_rows(partner)
    s1 = mean(pick(odd, s0), pick(odd, r0))
    s1_send = s1.astype(BF16)
    r1_half = swap(s1_send, 1, count)
    place, _ = after(info, s1_send)
    kernels, _ = after(kernels, s1_send)
    weights = pl.pallas_call(
        prep_kernel,
        out_shape=jax.ShapeDtypeStruct((BANDS, 7 * LANES, 2 * LANES), BF16),
        in_specs=[SMEM],
        out_specs=VMEM,
        scratch_shapes=[pltpu.VMEM((5, LANES, LANES), F32)],
        compiler_params=pltpu.CompilerParams(vmem_limit_bytes=4 << 20),
        cost_estimate=cost(1.5e9, 1e6),
        name="taps",
    )(kernels)
    regions = covariance.shape[1]
    chosen = pl.pallas_call(
        functools.partial(choose_kernel, levels, rows, blocks),
        out_shape=jax.ShapeDtypeStruct((BANDS, blocks, rows, 2 * LANES), BF16),
        in_specs=[SMEM, SMEM, VMEM],
        out_specs=VMEM,
        scratch_shapes=[pltpu.VMEM((rows * regions, LANES), F32)] * 2,
        compiler_params=pltpu.CompilerParams(vmem_limit_bytes=10 << 20),
        cost_estimate=cost(3e9, 6e6),
        name="choose",
    )(place, region, jnp.transpose(covariance, (0, 2, 1, 3)))
    sides = jnp.concatenate([edge(s0), mean(edge(s0), edge(r0)).astype(BF16)], 0)
    s2_part = mean(pick(second, s1), pick(second, r1_half))
    r2_part = swap(s2_part.astype(BF16), 2, count)
    r1 = gather(r1_half, 0, odd)
    s2_edge = mean(mean(edge(s0), edge(r0)), edge(r1)).astype(BF16)
    near = outer_swap(jnp.concatenate([sides, s2_edge], 0), 1, count)
    sides, _ = after(edge(s0), r1)
    across = outer_swap(sides, 0, count, only=True)
    middle = near[4:]
    s3_part = mean(s2_part, r2_part)
    r3_part = swap(s3_part.astype(BF16), 3, count)
    r2_half = gather(r2_part, 1, second)
    r3_part, (r2_half, across, near) = after(r3_part, (r2_half, across, near))
    r2 = gather(r2_half, 0, odd)
    middle = near[4:]
    h = {0: jnp.where(far == 1, across, near[:2]), 1: near[2:4], 2: middle}
    fine = filter_part((0, 1), info, s0, (r0, r1, r2_part), h, weights, "fine", 8e8)
    r3_half = gather(r3_part, 1, second)
    if count > 1 << LEVELS:
        s3_edge = mean(mean(mean(edge(s0), edge(r0)), edge(r1)), edge(r2))
        h[3] = outer_swap(s3_edge.astype(BF16), 3, count)
    third = filter_part((2,), info, s0, (r0, r1, r2, r3_part), h, weights, "third", 4e8)
    acc = pl.pallas_call(
        functools.partial(vertical_kernel, lons, blocks),
        out_shape=jax.ShapeDtypeStruct((blocks, rows, lons * LANES), F32),
        in_specs=[VMEM] * 3,
        out_specs=VMEM,
        compiler_params=pltpu.CompilerParams(vmem_limit_bytes=8 << 20),
        cost_estimate=cost(5e8, 1e6),
        name="vertical",
    )(chosen, fine, third)
    r3_half, acc = after(r3_half, acc)
    r3 = gather(r3_half, 0, odd)
    if count > 1 << LEVELS:
        s4_edge = mean(s3_edge, edge(r3))
        h[4] = outer_swap(s4_edge.astype(BF16), 3, count)
    out = filter_part((3, 4), info, s0, (r0, r1, r2, r3), h, weights, "last", 1e9, chosen, acc)
    return jnp.transpose(out[:, :levels], (1, 0, 2))


def solution(mesh):
    placed = (P(None, ("member", "lon"), None), P(), P(), P())
    return jax.shard_map(
        functools.partial(on_device, mesh.shape["lon"]),
        mesh=mesh,
        in_specs=placed,
        out_specs=P(None, ("member", "lon"), None),
        check_vma=False,
    )
```

time: 251 us -> 70.4 us (0.28)
  other arithmetic: 120 us -> 4.63 us
  waiting for transfers between devices: 80.2 us -> 28.6 us
  Pallas kernels: 0 us -> 16.7 us
  starting transfers between devices: 26.4 us -> 14.1 us
  local copies, waits for them, and re-layouts: 13 us -> 5.85 us
  between operations: 6.11 us -> 0.23 us
  matrix products: 3.29 us -> 0 us
    convert_element_type x9 -> x5, other arithmetic: 113 us -> 2.6 us  [the longest x1 1.18 us: on_device(): r2_part = swap(s2_part.astype(BF16), 2, count)]
    ppermute x14 -> x11, waiting for transfers between devices: 80.2 us -> 28.6 us  [the longest x9 28.6 us: swap(): return lax.ppermute(field, 'lon', [(t, t ^ 1 << bit) for t in range(count)])]
    pallas_call x0 -> x6, Pallas kernels: none -> 16.7 us  [the longest x3 11.7 us: filter_part(): pl.pallas_call(functools.partial(kernel, ks, lons, blocks, halos), out_sh...]
    ppermute x14 -> x11, starting transfers between devices: 26.4 us -> 14.1 us  [the longest x9 8.67 us: swap(): return lax.ppermute(field, 'lon', [(t, t ^ 1 << bit) for t in range(count)])]
    slice x14 -> x0, local copies, waits for them, and re-layouts: 7.71 us -> none  [the longest x7 6.41 us: filter_padded(): weights[row_shift * 5 + col_shift] * window.astype(jnp.float32)]
    concatenate x5 -> x6, other arithmetic: 5.28 us -> 0.51 us  [the longest x5 0.42 us: pair_up(): jnp.concatenate([jnp.where(which == 1, mine, other), jnp.where(which == 1...]
    unnamed x8, local copies, waits for them, and re-layouts: 0.25 us -> 4.39 us
    dot_general x15 -> x0, matrix products: 3.29 us -> none  [apply_blocks(): jnp.einsum('ab,bxr->axr', matrix, columns, preferred_element_type=jnp.flo...]
  transfers between devices with their start and end apart: 14 -> 11, of which waited for: 5 -> 6; matrix products, arithmetic and copies ran while one was open for 43% -> 7% of each run, Pallas kernels for 0% -> 12%
where the time goes in v2:
time: 70.4 us; the launch traced here: 70.1 us
  waiting for transfers between devices  28.6 us (41%)
  Pallas kernels  16.7 us (24%)
  starting transfers between devices  14.1 us (20%)
  local copies, waits for them, and re-layouts  5.85 us (8%)
  other arithmetic  4.63 us (7%)
    ppermute x9, waiting for transfers between devices, swap(): return lax.ppermute(field, 'lon', [(t, t ^ 1 << bit) for t in range(count)])  28.6 us
    pallas_call x3, Pallas kernels, filter_part(): pl.pallas_call(functools.partial(kernel, ks, lons, blocks, halos), out_sh...  11.7 us
    ppermute x9, starting transfers between devices, swap(): return lax.ppermute(field, 'lon', [(t, t ^ 1 << bit) for t in range(count)])  8.67 us
    ppermute x2, starting transfers between devices, outer_swap(): return lax.ppermute(edge, 'lon', route)  5.39 us
    unnamed x8, local copies, waits for them, and re-layouts  4.39 us
    pallas_call x1, Pallas kernels, on_device(): pl.pallas_call(functools.partial(choose_kernel, levels, rows, blocks), ou...  2.65 us
    pallas_call x1, Pallas kernels, on_device(): pl.pallas_call(prep_kernel, out_shape=jax.ShapeDtypeStruct((BANDS, 7 * LA...  1.5 us
  transfers between devices with their start and end apart: 11, of which 6 were waited for; matrix products, arithmetic and copies ran while one was open for 7% of the time, Pallas kernels for 12%

profile of v2, /device:TPU:0, one launch (start us, length us, event | category | flops | bytes accessed | tf_op | source)
XLA Modules:
  0.0 70.1 jit_solution(13213955552870840002)
XLA Ops:
  0.5 1.3 %copy.16 = bf16[137,8,384]{2,0,1:T(8,128)(2,1)S(1)} copy(bf16[137,8,384]{2,1,0:T(8,128)(2,1)} %param.4) | data formatting | bytes 1683456 | tf_op args[0]
  1.7 0.9 %collective-permute-done = bf16[137,8,384]{2,1,0:T(8,128)(2,1)S(1)} collective-permute-done((bf16[137,8,384]{2,1,0:T(8,128)(2,1)}, bf16[137,8,384]{2,1,0:T(8,128)(2,1)S(1)}, u32[]{:S(2)}, u32[]{:S(2)}) %collective-permute-start) | collective-permute-done | bytes 841760 | tf_op jit(solution)/shard_map/ppermute | solution.py:22
  2.8 1.0 %fusion.5 = (bf16[4,144,384]{2,1,0:T(8,128)(2,1)}, f32[4,144,384]{2,1,0:T(8,128)S(1)}) fusion(bf16[8,137,384]{2,1,0:T(8,128)(2,1)S(1)} %bitcast.13, bf16[8,137,384]{2,1,0:T(8,128)(2,1)S(1)} %bitcast.17, pred[]{:T(512)S(6)} %eq.19), kind=kLoop, calls=%fused_computation.34 | loop fusion | flops 1548288 | bytes 3010561 | tf_op jit(solution)/shard_map/convert_element_type | solution.py:298
  3.8 2.9 %collective-permute-start.1 = (bf16[4,144,384]{2,1,0:T(8,128)(2,1)}, bf16[4,144,384]{2,1,0:T(8,128)(2,1)}, u32[]{:S(2)}, u32[]{:S(2)}) collective-permute-start(bf16[4,144,384]{2,1,0:T(8,128)(2,1)} %get-tuple-element.27), channel_id=1, source_target_pairs={{0,2},{1,3},{2,0},{3,1},{4,6},{5,7},{6,4},{7,5},{8,10},{9,11},{10,... | collective-permute-start | bytes 1327112 | tf_op jit(solution)/shard_map/ppermute | solution.py:22
  7.6 1.5 %taps.1.refs_8_.refs_7_.refs_6_ = bf16[5,896,256]{2,1,0:T(8,128)(2,1)S(1)} custom-call(f32[5,25]{1,0:T(8,128)S(1)} %copy-done.1), custom_call_target="tpu_custom_call" | custom-call | flops 1500000000 | bytes 1000000 | tf_op jit(solution)/shard_map/taps/pallas_call | solution.py:302
  9.1 8.3 %collective-permute-done.1 = bf16[4,144,384]{2,1,0:T(8,128)(2,1)} collective-permute-done((bf16[4,144,384]{2,1,0:T(8,128)(2,1)}, bf16[4,144,384]{2,1,0:T(8,128)(2,1)}, u32[]{:S(2)}, u32[]{:S(2)}) %collective-permute-start.1) | collective-permute-done | bytes 442400 | tf_op jit(solution)/shard_map/ppermute | solution.py:22
  17.5 1.2 %fusion.3 = (bf16[2,144,384]{2,1,0:T(8,128)(2,1)S(1)}, f32[2,144,384]{2,1,0:T(8,128)S(1)}) fusion(bf16[4,144,384]{2,1,0:T(8,128)(2,1)} %collective-permute-done.1, f32[4,144,384]{2,1,0:T(8,128)S(1)} %get-tuple-element.28, pred[]{:T(512)S(6)} %eq.20), kind=kLoop, calls=%fused_computation.33 | loop fusion | flops 663552 | bytes 1990657 | tf_op jit(solution)/shard_map/convert_element_type | solution.py:325
  18.6 1.9 %collective-permute-start.3 = (bf16[2,144,384]{2,1,0:T(8,128)(2,1)S(1)}, bf16[2,144,384]{2,1,0:T(8,128)(2,1)S(1)}, u32[]{:S(2)}, u32[]{:S(2)}) collective-permute-start(bf16[2,144,384]{2,1,0:T(8,128)(2,1)S(1)} %get-tuple-element.25), channel_id=1, source_target_pairs={{0,4},{1,5},{2,6},{3,7},{4,0},{5,1},{6,2},{7,3},{8,12},{9,13},{10,... | collective-permute-start | bytes 663560 | tf_op jit(solution)/shard_map/ppermute | solution.py:22
  20.5 2.6 %copy-done = bf16[5,16,137,137]{3,1,2,0:T(8,128)(2,1)S(1)} copy-done((bf16[5,16,137,137]{3,1,2,0:T(8,128)(2,1)S(1)}, bf16[5,16,137,137]{3,1,2,0:T(8,128)(2,1)}, u32[]{:S(2)}) %copy-start) | copy-done | bytes 3003064
  23.1 2.6 %choose.1.cov.refs_7_ = bf16[5,3,144,256]{3,2,1,0:T(8,128)(2,1)S(1)} custom-call(s32[3]{0:T(128)S(1)} %pad_add_fusion.place.refs_0_, s32[16,3]{1,0:T(8,128)S(1)} %copy.11.region, bf16[5,137,16,137]{3,2,1,0:T(8,128)(2,1)S(1)} %bitcast.12), custom_call_target="tpu_custom_call" | custom-call | flops 3000000000 | bytes 6000000 | tf_op jit(solution)/shard_map/choose/pallas_call | solution.py:313
  25.8 0.9 %collective-permute-done.3.refs_4_ = bf16[2,144,384]{2,1,0:T(8,128)(2,1)S(1)} collective-permute-done((bf16[2,144,384]{2,1,0:T(8,128)(2,1)S(1)}, bf16[2,144,384]{2,1,0:T(8,128)(2,1)S(1)}, u32[]{:S(2)}, u32[]{:S(2)}) %collective-permute-start.3) | collective-permute-done | bytes 221216 | tf_op jit(solution)/shard_map/ppermute | solution.py:22
  26.6 1.7 %collective-permute-start.5 = (bf16[2,144,384]{2,1,0:T(8,128)(2,1)S(1)}, bf16[2,144,384]{2,1,0:T(8,128)(2,1)S(1)}, u32[]{:S(2)}, u32[]{:S(2)}) collective-permute-start(bf16[2,144,384]{2,1,0:T(8,128)(2,1)S(1)} %collective-permute-done.3.refs_4_), channel_id=1, source_target_pairs={{0,2},{1,3},{2,0},{3,1},{4,6},{5,7},{6,4},{7,5},{8,10},{9,11},{10,... | collective-permute-start | bytes 663560 | tf_op jit(solution)/shard_map/ppermute | solution.py:22
  28.3 1.1 %broadcast_select_fusion.4 = (bf16[4,144,384]{2,1,0:T(8,128)(2,1)S(1)}, bf16[4,144,384]{2,1,0:T(8,128)(2,1)S(1)}) fusion(bf16[4,144,384]{2,1,0:T(8,128)(2,1)} %collective-permute-done.1, bf16[4,144,384]{2,1,0:T(8,128)(2,1)S(1)} %collective-permute-done.2, pred[]{:T(512)S(6)} %eq.19), kind=kLoop, calls=%fused_computation.20 | loop fusion | flops 442368 | bytes 1769473 | tf_op jit(solution)/shard_map/jit(_where)/select_n | solution.py:277
  29.7 4.5 %collective-permute-start.7 = (bf16[6,144,384]{2,1,0:T(8,128)(2,1)S(1)}, bf16[6,144,384]{2,1,0:T(8,128)(2,1)S(1)}, u32[]{:S(2)}, u32[]{:S(2)}) collective-permute-start(bf16[6,144,384]{2,1,0:T(8,128)(2,1)S(1)} %pad_maximum_fusion.3), channel_id=1, source_target_pairs={{3,4},{4,3},{7,8},{8,7},{11,12},{12,11},{15,0},{0,15},{19,20},{20,... | collective-permute-start | bytes 1990664 | tf_op jit(solution)/shard_map/ppermute | solution.py:30
  34.5 0.9 %collective-permute-start.6 = (bf16[2,144,384]{2,1,0:T(8,128)(2,1)S(1)}, bf16[2,144,384]{2,1,0:T(8,128)(2,1)S(1)}, u32[]{:S(2)}, u32[]{:S(2)}) collective-permute-start(bf16[2,144,384]{2,1,0:T(8,128)(2,1)S(1)} %get-tuple-element.14), channel_id=1, source_target_pairs={{1,2},{2,1},{5,6},{6,5},{9,10},{10,9},{13,14},{14,13},{17,18},{18,... | collective-permute-start | bytes 663560 | tf_op jit(solution)/shard_map/ppermute | solution.py:30
  35.5 14.6 %collective-permute-done.4.refs_5_ = bf16[2,144,384]{2,1,0:T(8,128)(2,1)S(1)} collective-permute-done((bf16[2,144,384]{2,1,0:T(8,128)(2,1)S(1)}, bf16[2,144,384]{2,1,0:T(8,128)(2,1)S(1)}, u32[]{:S(2)}, u32[]{:S(2)}) %collective-permute-start.4) | collective-permute-done | bytes 221216 | tf_op jit(solution)/shard_map/ppermute | solution.py:22
  50.1 1.7 %collective-permute-start.9 = (bf16[2,144,384]{2,1,0:T(8,128)(2,1)S(1)}, bf16[2,144,384]{2,1,0:T(8,128)(2,1)S(1)}, u32[]{:S(2)}, u32[]{:S(2)}) collective-permute-start(bf16[2,144,384]{2,1,0:T(8,128)(2,1)S(1)} %collective-permute-done.4.refs_5_), channel_id=1, source_target_pairs={{0,2},{1,3},{2,0},{3,1},{4,6},{5,7},{6,4},{7,5},{8,10},{9,11},{10,... | collective-permute-start | bytes 663560 | tf_op jit(solution)/shard_map/ppermute | solution.py:22
  51.9 4.0 %fine.1.refs_0_ = bf16[2,3,4,144,256]{4,3,2,1,0:T(8,128)(2,1)S(1)} custom-call(s32[3]{0:T(128)S(1)} %pad_add_fusion.place.refs_0_, bf16[8,144,384]{2,1,0:T(8,128)(2,1)S(1)} %pad.7.refs_1_, bf16[8,144,384]{2,1,0:T(8,128)(2,1)S(1)} %pad.8.refs_2_, bf16[8,144,384]{2,1,0:T(8,128)(2,1)S(1)} %pad_maximum_fusion.refs_3_, ...), custom_call_target="tpu_custom_call" | custom-call | flops 800000000 | bytes 1000000 | tf_op jit(solution)/shard_map/fine/pallas_call | solution.py:244
  55.8 2.1 %collective-permute-done.9 = bf16[2,144,384]{2,1,0:T(8,128)(2,1)S(1)} collective-permute-done((bf16[2,144,384]{2,1,0:T(8,128)(2,1)S(1)}, bf16[2,144,384]{2,1,0:T(8,128)(2,1)S(1)}, u32[]{:S(2)}, u32[]{:S(2)}) %collective-permute-start.9) | collective-permute-done | bytes 221216 | tf_op jit(solution)/shard_map/ppermute | solution.py:22
  58.3 2.8 %third.1.refs_1_ = bf16[1,3,4,144,256]{4,3,2,1,0:T(8,128)(2,1)S(1)} custom-call(s32[3]{0:T(128)S(1)} %pad_add_fusion.place.refs_0_, bf16[8,144,384]{2,1,0:T(8,128)(2,1)S(1)} %pad.7.refs_1_, bf16[8,144,384]{2,1,0:T(8,128)(2,1)S(1)} %pad.8.refs_2_, bf16[8,144,384]{2,1,0:T(8,128)(2,1)S(1)} %pad_maximum_fusion.refs_3_, ...), custom_call_target="tpu_custom_call" | custom-call | flops 400000000 | bytes 1000000 | tf_op jit(solution)/shard_map/third/pallas_call | solution.py:244
  61.1 0.8 %vertical.1.refs_8_ = f32[3,144,1024]{2,1,0:T(8,128)S(1)} custom-call(bf16[5,3,144,256]{3,2,1,0:T(8,128)(2,1)S(1)} %choose.1.cov.refs_7_, bf16[2,3,4,144,256]{4,3,2,1,0:T(8,128)(2,1)S(1)} %fine.1.refs_0_, bf16[1,3,4,144,256]{4,3,2,1,0:T(8,128)(2,1)S(1)} %third.1.refs_1_), custom_call_target="tpu_custom_call" | custom-call | flops 500000000 | bytes 1000000 | tf_op jit(solution)/shard_map/vertical/pallas_call | solution.py:345
  62.0 1.8 %collective-permute-done.10 = bf16[4,144,384]{2,1,0:T(8,128)(2,1)S(1)} collective-permute-done((bf16[4,144,384]{2,1,0:T(8,128)(2,1)S(1)}, bf16[4,144,384]{2,1,0:T(8,128)(2,1)S(1)}, u32[]{:S(2)}, u32[]{:S(2)}) %collective-permute-start.10) | collective-permute-done | bytes 442400 | tf_op jit(solution)/shard_map/ppermute | solution.py:22
  64.0 4.9 %last.1 = bf16[8,144,384]{2,1,0:T(8,128)(2,1)S(1)} custom-call(s32[3]{0:T(128)S(1)} %pad_add_fusion.place.refs_0_, bf16[8,144,384]{2,1,0:T(8,128)(2,1)S(1)} %pad.7.refs_1_, bf16[8,144,384]{2,1,0:T(8,128)(2,1)S(1)} %pad.8.refs_2_, bf16[8,144,384]{2,1,0:T(8,128)(2,1)S(1)} %pad_maximum_fusion.refs_3_, bf16[8,144,384]{2,1,0:T(8,128)(2,1)S(1)} %pad_maximum_fusion.1.refs_4_, ...), custom_call_target="tpu_custom_call" | custom-call | flops 1000000000 | bytes 1000000 | tf_op jit(solution)/shard_map/last/pallas_call | solution.py:244
  69.0 1.1 %copy.12 = bf16[137,8,384]{2,1,0:T(8,128)(2,1)} copy(bf16[137,8,384]{2,0,1:T(8,128)(2,1)S(1)} %slice_bitcast_fusion) | data formatting | bytes 1683456 | tf_op jit(solution)/shard_map/transpose | solution.py:360
  (35 shorter events, 2.9 us)
Async XLA Ops:
  0.0 2.7 %collective-permute-start = (bf16[137,8,384]{2,1,0:T(8,128)(2,1)}, bf16[137,8,384]{2,1,0:T(8,128)(2,1)S(1)}, u32[]{:S(2)}, u32[]{:S(2)}) collective-permute-start(bf16[137,8,384]{2,1,0:T(8,128)(2,1)} %param.4), channel_id=1, source_target_pairs={{0,1},{1,0},{2,3},{3,2},{4,5},{5,4},{6,7},{7,6},{8,9},{9,8},{10,11... | collective-permute-start | bytes 2525192 | tf_op jit(solution)/shard_map/ppermute | solution.py:22
  2.8 4.0 %copy-start.2 = (s32[16,3]{0,1:T(4,128)S(1)}, s32[16,3]{0,1:T(4,128)}, u32[]{:S(2)}) copy-start(s32[16,3]{0,1:T(4,128)} %param.7) | copy-start | bytes 580
  3.8 13.6 %collective-permute-start.1 = (bf16[4,144,384]{2,1,0:T(8,128)(2,1)}, bf16[4,144,384]{2,1,0:T(8,128)(2,1)}, u32[]{:S(2)}, u32[]{:S(2)}) collective-permute-start(bf16[4,144,384]{2,1,0:T(8,128)(2,1)} %get-tuple-element.27), channel_id=1, source_target_pairs={{0,2},{1,3},{2,0},{3,1},{4,6},{5,7},{6,4},{7,5},{8,10},{9,11},{10,... | collective-permute-start | bytes 1327112 | tf_op jit(solution)/shard_map/ppermute | solution.py:22
  6.9 0.7 copy-start.1
  17.4 10.8 %collective-permute-start.2 = (bf16[4,144,384]{2,1,0:T(8,128)(2,1)}, bf16[4,144,384]{2,1,0:T(8,128)(2,1)S(1)}, u32[]{:S(2)}, u32[]{:S(2)}) collective-permute-start(bf16[4,144,384]{2,1,0:T(8,128)(2,1)} %collective-permute-done.1), channel_id=1, source_target_pairs={{0,1},{1,0},{2,3},{3,2},{4,5},{5,4},{6,7},{7,6},{8,9},{9,8},{10,11... | collective-permute-start | bytes 1327112 | tf_op jit(solution)/shard_map/ppermute | solution.py:22
  18.6 8.0 %collective-permute-start.3 = (bf16[2,144,384]{2,1,0:T(8,128)(2,1)S(1)}, bf16[2,144,384]{2,1,0:T(8,128)(2,1)S(1)}, u32[]{:S(2)}, u32[]{:S(2)}) collective-permute-start(bf16[2,144,384]{2,1,0:T(8,128)(2,1)S(1)} %get-tuple-element.25), channel_id=1, source_target_pairs={{0,4},{1,5},{2,6},{3,7},{4,0},{5,1},{6,2},{7,3},{8,12},{9,13},{10,... | collective-permute-start | bytes 663560 | tf_op jit(solution)/shard_map/ppermute | solution.py:22
  20.5 2.6 %copy-start = (bf16[5,16,137,137]{3,1,2,0:T(8,128)(2,1)S(1)}, bf16[5,16,137,137]{3,1,2,0:T(8,128)(2,1)}, u32[]{:S(2)}) copy-start(bf16[5,16,137,137]{3,1,2,0:T(8,128)(2,1)} %param.6) | copy-start | bytes 9009124
  26.6 8.7 %collective-permute-start.5 = (bf16[2,144,384]{2,1,0:T(8,128)(2,1)S(1)}, bf16[2,144,384]{2,1,0:T(8,128)(2,1)S(1)}, u32[]{:S(2)}, u32[]{:S(2)}) collective-permute-start(bf16[2,144,384]{2,1,0:T(8,128)(2,1)S(1)} %collective-permute-done.3.refs_4_), channel_id=1, source_target_pairs={{0,2},{1,3},{2,0},{3,1},{4,6},{5,7},{6,4},{7,5},{8,10},{9,11},{10,... | collective-permute-start | bytes 663560 | tf_op jit(solution)/shard_map/ppermute | solution.py:22
  29.7 20.4 %collective-permute-start.7 = (bf16[6,144,384]{2,1,0:T(8,128)(2,1)S(1)}, bf16[6,144,384]{2,1,0:T(8,128)(2,1)S(1)}, u32[]{:S(2)}, u32[]{:S(2)}) collective-permute-start(bf16[6,144,384]{2,1,0:T(8,128)(2,1)S(1)} %pad_maximum_fusion.3), channel_id=1, source_target_pairs={{3,4},{4,3},{7,8},{8,7},{11,12},{12,11},{15,0},{0,15},{19,20},{20,... | collective-permute-start | bytes 1990664 | tf_op jit(solution)/shard_map/ppermute | solution.py:30
  34.3 15.8 %collective-permute-start.4 = (bf16[2,144,384]{2,1,0:T(8,128)(2,1)S(1)}, bf16[2,144,384]{2,1,0:T(8,128)(2,1)S(1)}, u32[]{:S(2)}, u32[]{:S(2)}) collective-permute-start(bf16[2,144,384]{2,1,0:T(8,128)(2,1)S(1)} %multiply_convert_fusion.1), channel_id=1, source_target_pairs={{0,8},{1,9},{2,10},{3,11},{4,12},{5,13},{6,14},{7,15},{8,0},{9,1},... | collective-permute-start | bytes 663560 | tf_op jit(solution)/shard_map/ppermute | solution.py:22
  34.5 15.6 %collective-permute-start.6 = (bf16[2,144,384]{2,1,0:T(8,128)(2,1)S(1)}, bf16[2,144,384]{2,1,0:T(8,128)(2,1)S(1)}, u32[]{:S(2)}, u32[]{:S(2)}) collective-permute-start(bf16[2,144,384]{2,1,0:T(8,128)(2,1)S(1)} %get-tuple-element.14), channel_id=1, source_target_pairs={{1,2},{2,1},{5,6},{6,5},{9,10},{10,9},{13,14},{14,13},{17,18},{18,... | collective-permute-start | bytes 663560 | tf_op jit(solution)/shard_map/ppermute | solution.py:30
  50.1 8.0 %collective-permute-start.8 = (bf16[4,144,384]{2,1,0:T(8,128)(2,1)S(1)}, bf16[4,144,384]{2,1,0:T(8,128)(2,1)S(1)}, u32[]{:S(2)}, u32[]{:S(2)}) collective-permute-start(bf16[4,144,384]{2,1,0:T(8,128)(2,1)S(1)} %pad_maximum_fusion.4), channel_id=1, source_target_pairs={{0,1},{1,0},{2,3},{3,2},{4,5},{5,4},{6,7},{7,6},{8,9},{9,8},{10,11... | collective-permute-start | bytes 1327112 | tf_op jit(solution)/shard_map/ppermute | solution.py:22
  50.1 7.8 %collective-permute-start.9 = (bf16[2,144,384]{2,1,0:T(8,128)(2,1)S(1)}, bf16[2,144,384]{2,1,0:T(8,128)(2,1)S(1)}, u32[]{:S(2)}, u32[]{:S(2)}) collective-permute-start(bf16[2,144,384]{2,1,0:T(8,128)(2,1)S(1)} %collective-permute-done.4.refs_5_), channel_id=1, source_target_pairs={{0,2},{1,3},{2,0},{3,1},{4,6},{5,7},{6,4},{7,5},{8,10},{9,11},{10,... | collective-permute-start | bytes 663560 | tf_op jit(solution)/shard_map/ppermute | solution.py:22
  61.9 1.9 %collective-permute-start.10 = (bf16[4,144,384]{2,1,0:T(8,128)(2,1)S(1)}, bf16[4,144,384]{2,1,0:T(8,128)(2,1)S(1)}, u32[]{:S(2)}, u32[]{:S(2)}) collective-permute-start(bf16[4,144,384]{2,1,0:T(8,128)(2,1)S(1)} %pad_maximum_fusion.5), channel_id=1, source_target_pairs={{0,1},{1,0},{2,3},{3,2},{4,5},{5,4},{6,7},{7,6},{8,9},{9,8},{10,11... | collective-permute-start | bytes 1327112 | tf_op jit(solution)/shard_map/ppermute | solution.py:22

commit v3 on v2

--- a/solution.py
+++ b/solution.py
@@ -323,24 +323,25 @@
     sides = jnp.concatenate([edge(s0), mean(edge(s0), edge(r0)).astype(BF16)], 0)
     s2_part = mean(pick(second, s1), pick(second, r1_half))
     r2_part = swap(s2_part.astype(BF16), 2, count)
+    sides, _ = after(sides, weights)
+    near = outer_swap(sides, 1, count)
     r1 = gather(r1_half, 0, odd)
     s2_edge = mean(mean(edge(s0), edge(r0)), edge(r1)).astype(BF16)
-    near = outer_swap(jnp.concatenate([sides, s2_edge], 0), 1, count)
+    middle = outer_swap(s2_edge, 2, count)
     sides, _ = after(edge(s0), r1)
     across = outer_swap(sides, 0, count, only=True)
-    middle = near[4:]
     s3_part = mean(s2_part, r2_part)
     r3_part = swap(s3_part.astype(BF16), 3, count)
     r2_half = gather(r2_part, 1, second)
-    r3_part, (r2_half, across, near) = after(r3_part, (r2_half, across, near))
+    r3_part, (r2_half, across, middle) = after(r3_part, (r2_half, across, middle))
     r2 = gather(r2_half, 0, odd)
-    middle = near[4:]
-    h = {0: jnp.where(far == 1, across, near[:2]), 1: near[2:4], 2: middle}
+    h = {0: jnp.where(far == 1, across, near[:2]), 1: near[2:], 2: middle}
     fine = filter_part((0, 1), info, s0, (r0, r1, r2_part), h, weights, "fine", 8e8)
     r3_half = gather(r3_part, 1, second)
     if count > 1 << LEVELS:
         s3_edge = mean(mean(mean(edge(s0), edge(r0)), edge(r1)), edge(r2))
         h[3] = outer_swap(s3_edge.astype(BF16), 3, count)
+    r3_half, fine = after(r3_half, fine)
     third = filter_part((2,), info, s0, (r0, r1, r2, r3_part), h, weights, "third", 4e8)
     acc = pl.pallas_call(
         functools.partial(vertical_kernel, lons, blocks),
@@ -351,7 +352,6 @@
         cost_estimate=cost(5e8, 1e6),
         name="vertical",
     )(chosen, fine, third)
-    r3_half, acc = after(r3_half, acc)
     r3 = gather(r3_half, 0, odd)
     if count > 1 << LEVELS:
         s4_edge = mean(s3_edge, edge(r3))

time: 70.4 us -> 62.5 us (0.89)
  waiting for transfers between devices: 28.6 us -> 20.8 us
  starting transfers between devices: 14.1 us -> 20 us
  local copies, waits for them, and re-layouts: 5.85 us -> 2.84 us
  other arithmetic: 4.63 us -> 1.72 us
    ppermute x9, waiting for transfers between devices: 28.6 us -> 20.7 us  [swap(): return lax.ppermute(field, 'lon', [(t, t ^ 1 << bit) for t in range(count)])]
    ppermute x2 -> x3, starting transfers between devices: 5.39 us -> 8.5 us  [outer_swap(): return lax.ppermute(edge, 'lon', route)]
    unnamed x8 -> x10, local copies, waits for them, and re-layouts: 4.39 us -> 1.37 us
    ppermute x9, starting transfers between devices: 8.67 us -> 11.5 us  [swap(): return lax.ppermute(field, 'lon', [(t, t ^ 1 << bit) for t in range(count)])]
    convert_element_type x1, other arithmetic: 1.18 us -> 0.1 us  [on_device(): r2_part = swap(s2_part.astype(BF16), 2, count)]
    select_n x5, other arithmetic: 1.37 us -> 0.36 us  [pair_up(): jnp.where(which == 1, mine, other)]
    convert_element_type x1, other arithmetic: 1.02 us -> 0.26 us  [on_device(): s1_send = s1.astype(BF16)]
  transfers between devices with their start and end apart: 11 -> 12, of which waited for: 6 -> 5; matrix products, arithmetic and copies ran while one was open for 7% -> 4% of each run, Pallas kernels for 12% -> 13%
where the time goes in v3:
time: 62.5 us; the launch traced here: 62.3 us
  waiting for transfers between devices  20.8 us (33%)
  starting transfers between devices  20 us (32%)
  Pallas kernels  16.7 us (27%)
  local copies, waits for them, and re-layouts  2.84 us (5%)
  other arithmetic  1.72 us (3%)
    ppermute x9, waiting for transfers between devices, swap(): return lax.ppermute(field, 'lon', [(t, t ^ 1 << bit) for t in range(count)])  20.7 us
    pallas_call x3, Pallas kernels, filter_part(): pl.pallas_call(functools.partial(kernel, ks, lons, blocks, halos), out_sh...  11.7 us
    ppermute x9, starting transfers between devices, swap(): return lax.ppermute(field, 'lon', [(t, t ^ 1 << bit) for t in range(count)])  11.5 us
    ppermute x3, starting transfers between devices, outer_swap(): return lax.ppermute(edge, 'lon', route)  8.5 us
    pallas_call x1, Pallas kernels, on_device(): pl.pallas_call(functools.partial(choose_kernel, levels, rows, blocks), ou...  2.65 us
    pallas_call x1, Pallas kernels, on_device(): pl.pallas_call(prep_kernel, out_shape=jax.ShapeDtypeStruct((BANDS, 7 * LA...  1.5 us
    unnamed x10, local copies, waits for them, and re-layouts  1.37 us
  transfers between devices with their start and end apart: 12, of which 5 were waited for; matrix products, arithmetic and copies ran while one was open for 4% of the time, Pallas kernels for 13%

profile of v3, /device:TPU:0, one launch (start us, length us, event | category | flops | bytes accessed | tf_op | source)
XLA Modules:
  0.0 62.3 jit_solution(4467774900286874710)
XLA Ops:
  0.0 0.5 collective-permute-start
  0.5 1.3 %copy.16 = bf16[137,8,384]{2,0,1:T(8,128)(2,1)S(1)} copy(bf16[137,8,384]{2,1,0:T(8,128)(2,1)} %param.4) | data formatting | bytes 1683456 | tf_op args[0]
  1.7 0.9 %collective-permute-done = bf16[137,8,384]{2,1,0:T(8,128)(2,1)S(1)} collective-permute-done((bf16[137,8,384]{2,1,0:T(8,128)(2,1)}, bf16[137,8,384]{2,1,0:T(8,128)(2,1)S(1)}, u32[]{:S(2)}, u32[]{:S(2)}) %collective-permute-start) | collective-permute-done | bytes 841760 | tf_op jit(solution)/shard_map/ppermute | solution.py:22
  2.8 0.3 fusion.5
  3.1 2.9 %collective-permute-start.1 = (bf16[4,144,384]{2,1,0:T(8,128)(2,1)S(1)}, bf16[4,144,384]{2,1,0:T(8,128)(2,1)S(1)}, u32[]{:S(2)}, u32[]{:S(2)}) collective-permute-start(bf16[4,144,384]{2,1,0:T(8,128)(2,1)S(1)} %get-tuple-element.29), channel_id=1, source_target_pairs={{0,2},{1,3},{2,0},{3,1},{4,6},{5,7},{6,4},{7,5},{8,10},{9,11},{10,... | collective-permute-start | bytes 1327112 | tf_op jit(solution)/shard_map/ppermute | solution.py:22
  6.4 10.1 %collective-permute-done.1 = bf16[4,144,384]{2,1,0:T(8,128)(2,1)S(1)} collective-permute-done((bf16[4,144,384]{2,1,0:T(8,128)(2,1)S(1)}, bf16[4,144,384]{2,1,0:T(8,128)(2,1)S(1)}, u32[]{:S(2)}, u32[]{:S(2)}) %collective-permute-start.1) | collective-permute-done | bytes 442400 | tf_op jit(solution)/shard_map/ppermute | solution.py:22
  16.6 1.9 %collective-permute-start.3 = (bf16[2,144,384]{2,1,0:T(8,128)(2,1)S(1)}, bf16[2,144,384]{2,1,0:T(8,128)(2,1)S(1)}, u32[]{:S(2)}, u32[]{:S(2)}) collective-permute-start(bf16[2,144,384]{2,1,0:T(8,128)(2,1)S(1)} %get-tuple-element.27), channel_id=1, source_target_pairs={{0,4},{1,5},{2,6},{3,7},{4,0},{5,1},{6,2},{7,3},{8,12},{9,13},{10,... | collective-permute-start | bytes 663560 | tf_op jit(solution)/shard_map/ppermute | solution.py:22
  18.6 1.5 %taps.1.refs_8_.refs_7_.refs_6_ = bf16[5,896,256]{2,1,0:T(8,128)(2,1)S(1)} custom-call(f32[5,25]{1,0:T(8,128)S(1)} %copy-done), custom_call_target="tpu_custom_call" | custom-call | flops 1500000000 | bytes 1000000 | tf_op jit(solution)/shard_map/taps/pallas_call | solution.py:302
  20.1 5.4 %collective-permute-start.10 = (bf16[4,144,384]{2,1,0:T(8,128)(2,1)S(1)}, bf16[4,144,384]{2,1,0:T(8,128)(2,1)S(1)}, u32[]{:S(2)}, u32[]{:S(2)}) collective-permute-start(bf16[4,144,384]{2,1,0:T(8,128)(2,1)S(1)} %pad_maximum_fusion.5), channel_id=1, source_target_pairs={{3,4},{4,3},{7,8},{8,7},{11,12},{12,11},{15,0},{0,15},{19,20},{20,... | collective-permute-start | bytes 1327112 | tf_op jit(solution)/shard_map/ppermute | solution.py:30
  25.7 0.6 collective-permute-start.4
  26.3 1.5 %collective-permute-start.5 = (bf16[2,144,384]{2,1,0:T(8,128)(2,1)S(1)}, bf16[2,144,384]{2,1,0:T(8,128)(2,1)S(1)}, u32[]{:S(2)}, u32[]{:S(2)}) collective-permute-start(bf16[2,144,384]{2,1,0:T(8,128)(2,1)S(1)} %collective-permute-done.3.refs_4_), channel_id=1, source_target_pairs={{0,2},{1,3},{2,0},{3,1},{4,6},{5,7},{6,4},{7,5},{8,10},{9,11},{10,... | collective-permute-start | bytes 663560 | tf_op jit(solution)/shard_map/ppermute | solution.py:22
  28.1 0.7 %collective-permute-start.6 = (bf16[2,144,384]{2,1,0:T(8,128)(2,1)S(1)}, bf16[2,144,384]{2,1,0:T(8,128)(2,1)S(1)}, u32[]{:S(2)}, u32[]{:S(2)}) collective-permute-start(bf16[2,144,384]{2,1,0:T(8,128)(2,1)S(1)} %get-tuple-element.15), channel_id=1, source_target_pairs={{1,2},{2,1},{5,6},{6,5},{9,10},{10,9},{13,14},{14,13},{17,18},{18,... | collective-permute-start | bytes 663560 | tf_op jit(solution)/shard_map/ppermute | solution.py:30
  28.8 2.4 %collective-permute-start.7 = (bf16[2,144,384]{2,1,0:T(8,128)(2,1)S(1)}, bf16[2,144,384]{2,1,0:T(8,128)(2,1)S(1)}, u32[]{:S(2)}, u32[]{:S(2)}) collective-permute-start(bf16[2,144,384]{2,1,0:T(8,128)(2,1)S(1)} %multiply_convert_fusion), channel_id=1, source_target_pairs={{7,8},{8,7},{15,0},{0,15},{23,24},{24,23},{31,16},{16,31}} | collective-permute-start | bytes 663560 | tf_op jit(solution)/shard_map/ppermute | solution.py:30
  31.2 5.6 %collective-permute-done.5 = bf16[2,144,384]{2,1,0:T(8,128)(2,1)S(1)} collective-permute-done((bf16[2,144,384]{2,1,0:T(8,128)(2,1)S(1)}, bf16[2,144,384]{2,1,0:T(8,128)(2,1)S(1)}, u32[]{:S(2)}, u32[]{:S(2)}) %collective-permute-start.5) | collective-permute-done | bytes 221216 | tf_op jit(solution)/shard_map/ppermute | solution.py:22
  37.0 3.3 %collective-permute-done.4.refs_5_ = bf16[2,144,384]{2,1,0:T(8,128)(2,1)S(1)} collective-permute-done((bf16[2,144,384]{2,1,0:T(8,128)(2,1)S(1)}, bf16[2,144,384]{2,1,0:T(8,128)(2,1)S(1)}, u32[]{:S(2)}, u32[]{:S(2)}) %collective-permute-start.4) | collective-permute-done | bytes 221216 | tf_op jit(solution)/shard_map/ppermute | solution.py:22
  40.3 4.1 %collective-permute-start.9 = (bf16[2,144,384]{2,1,0:T(8,128)(2,1)S(1)}, bf16[2,144,384]{2,1,0:T(8,128)(2,1)S(1)}, u32[]{:S(2)}, u32[]{:S(2)}) collective-permute-start(bf16[2,144,384]{2,1,0:T(8,128)(2,1)S(1)} %collective-permute-done.4.refs_5_), channel_id=1, source_target_pairs={{0,2},{1,3},{2,0},{3,1},{4,6},{5,7},{6,4},{7,5},{8,10},{9,11},{10,... | collective-permute-start | bytes 663560 | tf_op jit(solution)/shard_map/ppermute | solution.py:22
  44.5 4.0 %fine.1.refs_0_ = bf16[2,3,4,144,256]{4,3,2,1,0:T(8,128)(2,1)S(1)} custom-call(s32[3]{0:T(128)S(1)} %pad_add_fusion.refs_0_.place, bf16[8,144,384]{2,1,0:T(8,128)(2,1)S(1)} %pad.7.refs_1_, bf16[8,144,384]{2,1,0:T(8,128)(2,1)S(1)} %pad.8.refs_2_, bf16[8,144,384]{2,1,0:T(8,128)(2,1)S(1)} %pad_maximum_fusion.refs_3_, ...), custom_call_target="tpu_custom_call" | custom-call | flops 800000000 | bytes 1000000 | tf_op jit(solution)/shard_map/fine/pallas_call | solution.py:244
  48.5 0.8 %collective-permute-done.9 = bf16[2,144,384]{2,1,0:T(8,128)(2,1)S(1)} collective-permute-done((bf16[2,144,384]{2,1,0:T(8,128)(2,1)S(1)}, bf16[2,144,384]{2,1,0:T(8,128)(2,1)S(1)}, u32[]{:S(2)}, u32[]{:S(2)}) %collective-permute-start.9) | collective-permute-done | bytes 221216 | tf_op jit(solution)/shard_map/ppermute | solution.py:22
  49.5 2.6 %choose.1.cov.refs_7_ = bf16[5,3,144,256]{3,2,1,0:T(8,128)(2,1)S(1)} custom-call(s32[3]{0:T(128)S(1)} %pad_add_fusion.refs_0_.place, s32[16,3]{1,0:T(8,128)S(1)} %copy.11.region, bf16[5,137,16,137]{3,2,1,0:T(8,128)(2,1)S(1)} %bitcast.14), custom_call_target="tpu_custom_call" | custom-call | flops 3000000000 | bytes 6000000 | tf_op jit(solution)/shard_map/choose/pallas_call | solution.py:313
  52.4 0.2 pad_maximum_fusion.1
  52.6 2.8 %third.1.refs_1_ = bf16[1,3,4,144,256]{4,3,2,1,0:T(8,128)(2,1)S(1)} custom-call(s32[3]{0:T(128)S(1)} %pad_add_fusion.refs_0_.place, bf16[8,144,384]{2,1,0:T(8,128)(2,1)S(1)} %pad.7.refs_1_, bf16[8,144,384]{2,1,0:T(8,128)(2,1)S(1)} %pad.8.refs_2_, bf16[8,144,384]{2,1,0:T(8,128)(2,1)S(1)} %pad_maximum_fusion.refs_3_, ...), custom_call_target="tpu_custom_call" | custom-call | flops 400000000 | bytes 1000000 | tf_op jit(solution)/shard_map/third/pallas_call | solution.py:244
  55.4 0.8 %vertical.1.refs_8_ = f32[3,144,1024]{2,1,0:T(8,128)S(1)} custom-call(bf16[5,3,144,256]{3,2,1,0:T(8,128)(2,1)S(1)} %choose.1.cov.refs_7_, bf16[2,3,4,144,256]{4,3,2,1,0:T(8,128)(2,1)S(1)} %fine.1.refs_0_, bf16[1,3,4,144,256]{4,3,2,1,0:T(8,128)(2,1)S(1)} %third.1.refs_1_), custom_call_target="tpu_custom_call" | custom-call | flops 500000000 | bytes 1000000 | tf_op jit(solution)/shard_map/vertical/pallas_call | solution.py:346
  56.2 4.9 %last.1 = bf16[8,144,384]{2,1,0:T(8,128)(2,1)S(1)} custom-call(s32[3]{0:T(128)S(1)} %pad_add_fusion.refs_0_.place, bf16[8,144,384]{2,1,0:T(8,128)(2,1)S(1)} %pad.7.refs_1_, bf16[8,144,384]{2,1,0:T(8,128)(2,1)S(1)} %pad.8.refs_2_, bf16[8,144,384]{2,1,0:T(8,128)(2,1)S(1)} %pad_maximum_fusion.refs_3_, bf16[8,144,384]{2,1,0:T(8,128)(2,1)S(1)} %get-tuple-element.43.refs_4_, ...), custom_call_target="tpu_custom_call" | custom-call | flops 1000000000 | bytes 1000000 | tf_op jit(solution)/shard_map/last/pallas_call | solution.py:244
  61.2 1.1 %copy.12 = bf16[137,8,384]{2,1,0:T(8,128)(2,1)} copy(bf16[137,8,384]{2,0,1:T(8,128)(2,1)S(1)} %slice_bitcast_fusion) | data formatting | bytes 1683456 | tf_op jit(solution)/shard_map/transpose | solution.py:360
  (39 shorter events, 1.9 us)
Async XLA Ops:
  0.0 2.7 %collective-permute-start = (bf16[137,8,384]{2,1,0:T(8,128)(2,1)}, bf16[137,8,384]{2,1,0:T(8,128)(2,1)S(1)}, u32[]{:S(2)}, u32[]{:S(2)}) collective-permute-start(bf16[137,8,384]{2,1,0:T(8,128)(2,1)} %param.4), channel_id=1, source_target_pairs={{0,1},{1,0},{2,3},{3,2},{4,5},{5,4},{6,7},{7,6},{8,9},{9,8},{10,11... | collective-permute-start | bytes 2525192 | tf_op jit(solution)/shard_map/ppermute | solution.py:22
  2.8 3.2 %copy-start.1 = (s32[16,3]{0,1:T(4,128)S(1)}, s32[16,3]{0,1:T(4,128)}, u32[]{:S(2)}) copy-start(s32[16,3]{0,1:T(4,128)} %param.7) | copy-start | bytes 580
  3.1 13.4 %collective-permute-start.1 = (bf16[4,144,384]{2,1,0:T(8,128)(2,1)S(1)}, bf16[4,144,384]{2,1,0:T(8,128)(2,1)S(1)}, u32[]{:S(2)}, u32[]{:S(2)}) collective-permute-start(bf16[4,144,384]{2,1,0:T(8,128)(2,1)S(1)} %get-tuple-element.29), channel_id=1, source_target_pairs={{0,2},{1,3},{2,0},{3,1},{4,6},{5,7},{6,4},{7,5},{8,10},{9,11},{10,... | collective-permute-start | bytes 1327112 | tf_op jit(solution)/shard_map/ppermute | solution.py:22
  16.6 2.1 %copy-start = (f32[5,25]{1,0:T(8,128)S(1)}, f32[5,25]{1,0:T(8,128)}, u32[]{:S(2)}) copy-start(f32[5,25]{1,0:T(8,128)} %taps.2) | copy-start | bytes 1504
  16.6 9.0 %collective-permute-start.3 = (bf16[2,144,384]{2,1,0:T(8,128)(2,1)S(1)}, bf16[2,144,384]{2,1,0:T(8,128)(2,1)S(1)}, u32[]{:S(2)}, u32[]{:S(2)}) collective-permute-start(bf16[2,144,384]{2,1,0:T(8,128)(2,1)S(1)} %get-tuple-element.27), channel_id=1, source_target_pairs={{0,4},{1,5},{2,6},{3,7},{4,0},{5,1},{6,2},{7,3},{8,12},{9,13},{10,... | collective-permute-start | bytes 663560 | tf_op jit(solution)/shard_map/ppermute | solution.py:22
  18.5 9.3 %collective-permute-start.2 = (bf16[4,144,384]{2,1,0:T(8,128)(2,1)S(1)}, bf16[4,144,384]{2,1,0:T(8,128)(2,1)S(1)}, u32[]{:S(2)}, u32[]{:S(2)}) collective-permute-start(bf16[4,144,384]{2,1,0:T(8,128)(2,1)S(1)} %collective-permute-done.1), channel_id=1, source_target_pairs={{0,1},{1,0},{2,3},{3,2},{4,5},{5,4},{6,7},{7,6},{8,9},{9,8},{10,11... | collective-permute-start | bytes 1327112 | tf_op jit(solution)/shard_map/ppermute | solution.py:22
  20.1 24.2 %collective-permute-start.10 = (bf16[4,144,384]{2,1,0:T(8,128)(2,1)S(1)}, bf16[4,144,384]{2,1,0:T(8,128)(2,1)S(1)}, u32[]{:S(2)}, u32[]{:S(2)}) collective-permute-start(bf16[4,144,384]{2,1,0:T(8,128)(2,1)S(1)} %pad_maximum_fusion.5), channel_id=1, source_target_pairs={{3,4},{4,3},{7,8},{8,7},{11,12},{12,11},{15,0},{0,15},{19,20},{20,... | collective-permute-start | bytes 1327112 | tf_op jit(solution)/shard_map/ppermute | solution.py:30
  25.7 14.6 %collective-permute-start.4 = (bf16[2,144,384]{2,1,0:T(8,128)(2,1)S(1)}, bf16[2,144,384]{2,1,0:T(8,128)(2,1)S(1)}, u32[]{:S(2)}, u32[]{:S(2)}) collective-permute-start(bf16[2,144,384]{2,1,0:T(8,128)(2,1)S(1)} %multiply_convert_fusion.1), channel_id=1, source_target_pairs={{0,8},{1,9},{2,10},{3,11},{4,12},{5,13},{6,14},{7,15},{8,0},{9,1},... | collective-permute-start | bytes 663560 | tf_op jit(solution)/shard_map/ppermute | solution.py:22
  26.3 10.6 %collective-permute-start.5 = (bf16[2,144,384]{2,1,0:T(8,128)(2,1)S(1)}, bf16[2,144,384]{2,1,0:T(8,128)(2,1)S(1)}, u32[]{:S(2)}, u32[]{:S(2)}) collective-permute-start(bf16[2,144,384]{2,1,0:T(8,128)(2,1)S(1)} %collective-permute-done.3.refs_4_), channel_id=1, source_target_pairs={{0,2},{1,3},{2,0},{3,1},{4,6},{5,7},{6,4},{7,5},{8,10},{9,11},{10,... | collective-permute-start | bytes 663560 | tf_op jit(solution)/shard_map/ppermute | solution.py:22
  28.1 12.1 %collective-permute-start.6 = (bf16[2,144,384]{2,1,0:T(8,128)(2,1)S(1)}, bf16[2,144,384]{2,1,0:T(8,128)(2,1)S(1)}, u32[]{:S(2)}, u32[]{:S(2)}) collective-permute-start(bf16[2,144,384]{2,1,0:T(8,128)(2,1)S(1)} %get-tuple-element.15), channel_id=1, source_target_pairs={{1,2},{2,1},{5,6},{6,5},{9,10},{10,9},{13,14},{14,13},{17,18},{18,... | collective-permute-start | bytes 663560 | tf_op jit(solution)/shard_map/ppermute | solution.py:30
  28.8 11.5 %collective-permute-start.7 = (bf16[2,144,384]{2,1,0:T(8,128)(2,1)S(1)}, bf16[2,144,384]{2,1,0:T(8,128)(2,1)S(1)}, u32[]{:S(2)}, u32[]{:S(2)}) collective-permute-start(bf16[2,144,384]{2,1,0:T(8,128)(2,1)S(1)} %multiply_convert_fusion), channel_id=1, source_target_pairs={{7,8},{8,7},{15,0},{0,15},{23,24},{24,23},{31,16},{16,31}} | collective-permute-start | bytes 663560 | tf_op jit(solution)/shard_map/ppermute | solution.py:30
  40.3 9.0 %collective-permute-start.9 = (bf16[2,144,384]{2,1,0:T(8,128)(2,1)S(1)}, bf16[2,144,384]{2,1,0:T(8,128)(2,1)S(1)}, u32[]{:S(2)}, u32[]{:S(2)}) collective-permute-start(bf16[2,144,384]{2,1,0:T(8,128)(2,1)S(1)} %collective-permute-done.4.refs_5_), channel_id=1, source_target_pairs={{0,2},{1,3},{2,0},{3,1},{4,6},{5,7},{6,4},{7,5},{8,10},{9,11},{10,... | collective-permute-start | bytes 663560 | tf_op jit(solution)/shard_map/ppermute | solution.py:22
  44.4 7.8 %collective-permute-start.8 = (bf16[4,144,384]{2,1,0:T(8,128)(2,1)S(1)}, bf16[4,144,384]{2,1,0:T(8,128)(2,1)S(1)}, u32[]{:S(2)}, u32[]{:S(2)}) collective-permute-start(bf16[4,144,384]{2,1,0:T(8,128)(2,1)S(1)} %pad_maximum_fusion.3), channel_id=1, source_target_pairs={{0,1},{1,0},{2,3},{3,2},{4,5},{5,4},{6,7},{7,6},{8,9},{9,8},{10,11... | collective-permute-start | bytes 1327112 | tf_op jit(solution)/shard_map/ppermute | solution.py:22
  44.4 5.1 %slice-start = ((s8[5611520]{0:T(1024)(128)(4,1)}), s8[4194304]{0:T(1024)(128)(4,1)S(1)}, s32[]{:S(2)}) async-start(s8[5611520]{0:T(1024)(128)(4,1)} %bitcast.12), calls=%async_computation | async-start | bytes 8388608
  44.4 5.1 %slice-start.1 = ((s8[5611520]{0:T(1024)(128)(4,1)}), s8[1417216]{0:T(1024)(128)(4,1)S(1)}, s32[]{:S(2)}) async-start(s8[5611520]{0:T(1024)(128)(4,1)} %bitcast.12), calls=%async_computation.1 | async-start | bytes 2834432
  49.4 2.9 %collective-permute-start.11 = (bf16[4,144,384]{2,1,0:T(8,128)(2,1)S(1)}, bf16[4,144,384]{2,1,0:T(8,128)(2,1)S(1)}, u32[]{:S(2)}, u32[]{:S(2)}) collective-permute-start(bf16[4,144,384]{2,1,0:T(8,128)(2,1)S(1)} %pad_maximum_fusion.4), channel_id=1, source_target_pairs={{0,1},{1,0},{2,3},{3,2},{4,5},{5,4},{6,7},{7,6},{8,9},{9,8},{10,11... | collective-permute-start | bytes 1327112 | tf_op jit(solution)/shard_map/ppermute | solution.py:22

commit v4 on v3

--- a/solution.py
+++ b/solution.py
@@ -322,6 +322,7 @@
     )(place, region, jnp.transpose(covariance, (0, 2, 1, 3)))
     sides = jnp.concatenate([edge(s0), mean(edge(s0), edge(r0)).astype(BF16)], 0)
     s2_part = mean(pick(second, s1), pick(second, r1_half))
+    s2_part, (chosen, weights) = after(s2_part, (chosen, weights))
     r2_part = swap(s2_part.astype(BF16), 2, count)
     sides, _ = after(sides, weights)
     near = outer_swap(sides, 1, count)
@@ -341,8 +342,8 @@
     if count > 1 << LEVELS:
         s3_edge = mean(mean(mean(edge(s0), edge(r0)), edge(r1)), edge(r2))
         h[3] = outer_swap(s3_edge.astype(BF16), 3, count)
-    r3_half, fine = after(r3_half, fine)
     third = filter_part((2,), info, s0, (r0, r1, r2, r3_part), h, weights, "third", 4e8)
+    r3_half, (fine, third) = after(r3_half, (fine, third))
     acc = pl.pallas_call(
         functools.partial(vertical_kernel, lons, blocks),
         out_shape=jax.ShapeDtypeStruct((blocks, rows, lons * LANES), F32),

time: 62.5 us -> 60.7 us (0.971)
  waiting for transfers between devices: 20.8 us -> 16.4 us
  starting transfers between devices: 20 us -> 21.5 us
  local copies, waits for them, and re-layouts: 2.84 us -> 3.8 us
    ppermute x9, waiting for transfers between devices: 20.7 us -> 16.4 us  [swap(): return lax.ppermute(field, 'lon', [(t, t ^ 1 << bit) for t in range(count)])]
    ppermute x9, starting transfers between devices: 11.5 us -> 13.3 us  [swap(): return lax.ppermute(field, 'lon', [(t, t ^ 1 << bit) for t in range(count)])]
    unnamed x10 -> x8, local copies, waits for them, and re-layouts: 1.37 us -> 2.34 us
  transfers between devices with their start and end apart: 12 -> 12, of which waited for: 5 -> 6; matrix products, arithmetic and copies ran while one was open for 4% -> 4% of each run, Pallas kernels for 13% -> 15%
where the time goes in v4:
time: 60.7 us; the launch traced here: 60.4 us
  starting transfers between devices  21.5 us (35%)
  Pallas kernels  16.7 us (28%)
  waiting for transfers between devices  16.4 us (27%)
  local copies, waits for them, and re-layouts  3.8 us (6%)
  other arithmetic  1.72 us (3%)
    ppermute x9, waiting for transfers between devices, swap(): return lax.ppermute(field, 'lon', [(t, t ^ 1 << bit) for t in range(count)])  16.4 us
    ppermute x9, starting transfers between devices, swap(): return lax.ppermute(field, 'lon', [(t, t ^ 1 << bit) for t in range(count)])  13.3 us
    pallas_call x3, Pallas kernels, filter_part(): pl.pallas_call(functools.partial(kernel, ks, lons, blocks, halos), out_sh...  11.7 us
    ppermute x3, starting transfers between devices, outer_swap(): return lax.ppermute(edge, 'lon', route)  8.2 us
    pallas_call x1, Pallas kernels, on_device(): pl.pallas_call(functools.partial(choose_kernel, levels, rows, blocks), ou...  2.65 us
    unnamed x8, local copies, waits for them, and re-layouts  2.34 us
    pallas_call x1, Pallas kernels, on_device(): pl.pallas_call(prep_kernel, out_shape=jax.ShapeDtypeStruct((BANDS, 7 * LA...  1.5 us
  transfers between devices with their start and end apart: 12, of which 6 were waited for; matrix products, arithmetic and copies ran while one was open for 4% of the time, Pallas kernels for 15%

profile of v4, /device:TPU:0, one launch (start us, length us, event | category | flops | bytes accessed | tf_op | source)
XLA Modules:
  0.0 60.4 jit_solution(17478480290416608414)
XLA Ops:
  0.5 1.3 %copy.16 = bf16[137,8,384]{2,0,1:T(8,128)(2,1)S(1)} copy(bf16[137,8,384]{2,1,0:T(8,128)(2,1)} %param.4) | data formatting | bytes 1683456 | tf_op args[0]
  1.8 0.9 %collective-permute-done = bf16[137,8,384]{2,1,0:T(8,128)(2,1)S(1)} collective-permute-done((bf16[137,8,384]{2,1,0:T(8,128)(2,1)}, bf16[137,8,384]{2,1,0:T(8,128)(2,1)S(1)}, u32[]{:S(2)}, u32[]{:S(2)}) %collective-permute-start) | collective-permute-done | bytes 841760 | tf_op jit(solution)/shard_map/ppermute | solution.py:22
  3.1 2.9 %collective-permute-start.1 = (bf16[4,144,384]{2,1,0:T(8,128)(2,1)S(1)}, bf16[4,144,384]{2,1,0:T(8,128)(2,1)S(1)}, u32[]{:S(2)}, u32[]{:S(2)}) collective-permute-start(bf16[4,144,384]{2,1,0:T(8,128)(2,1)S(1)} %get-tuple-element.35), channel_id=1, source_target_pairs={{0,2},{1,3},{2,0},{3,1},{4,6},{5,7},{6,4},{7,5},{8,10},{9,11},{10,... | collective-permute-start | bytes 1327112 | tf_op jit(solution)/shard_map/ppermute | solution.py:22
  6.4 0.5 copy-done.1
  6.8 1.5 %taps.1.refs_8_.refs_7_.refs_6_ = bf16[5,896,256]{2,1,0:T(8,128)(2,1)S(1)} custom-call(f32[5,25]{1,0:T(8,128)S(1)} %copy-done.1), custom_call_target="tpu_custom_call" | custom-call | flops 1500000000 | bytes 1000000 | tf_op jit(solution)/shard_map/taps/pallas_call | solution.py:302
  8.3 0.5 copy-done
  8.8 2.6 %choose.1.cov.refs_7_ = bf16[5,3,144,256]{3,2,1,0:T(8,128)(2,1)S(1)} custom-call(s32[3]{0:T(128)S(1)} %pad_add_fusion.place.refs_0_, s32[16,3]{1,0:T(8,128)S(1)} %copy.11.region, bf16[5,137,16,137]{3,2,1,0:T(8,128)(2,1)S(1)} %bitcast.12), custom_call_target="tpu_custom_call" | custom-call | flops 3000000000 | bytes 6000000 | tf_op jit(solution)/shard_map/choose/pallas_call | solution.py:313
  11.5 5.0 %collective-permute-done.1 = bf16[4,144,384]{2,1,0:T(8,128)(2,1)S(1)} collective-permute-done((bf16[4,144,384]{2,1,0:T(8,128)(2,1)S(1)}, bf16[4,144,384]{2,1,0:T(8,128)(2,1)S(1)}, u32[]{:S(2)}, u32[]{:S(2)}) %collective-permute-start.1) | collective-permute-done | bytes 442400 | tf_op jit(solution)/shard_map/ppermute | solution.py:22
  16.6 1.9 %collective-permute-start.3 = (bf16[2,144,384]{2,1,0:T(8,128)(2,1)S(1)}, bf16[2,144,384]{2,1,0:T(8,128)(2,1)S(1)}, u32[]{:S(2)}, u32[]{:S(2)}) collective-permute-start(bf16[2,144,384]{2,1,0:T(8,128)(2,1)S(1)} %convert_element_type.45), channel_id=1, source_target_pairs={{0,4},{1,5},{2,6},{3,7},{4,0},{5,1},{6,2},{7,3},{8,12},{9,13},{10,... | collective-permute-start | bytes 663560 | tf_op jit(solution)/shard_map/ppermute | solution.py:22
  18.7 5.4 %collective-permute-start.10 = (bf16[4,144,384]{2,1,0:T(8,128)(2,1)S(1)}, bf16[4,144,384]{2,1,0:T(8,128)(2,1)S(1)}, u32[]{:S(2)}, u32[]{:S(2)}) collective-permute-start(bf16[4,144,384]{2,1,0:T(8,128)(2,1)S(1)} %pad_maximum_fusion.5), channel_id=1, source_target_pairs={{3,4},{4,3},{7,8},{8,7},{11,12},{12,11},{15,0},{0,15},{19,20},{20,... | collective-permute-start | bytes 1327112 | tf_op jit(solution)/shard_map/ppermute | solution.py:30
  24.2 2.1 %collective-permute-start.4 = (bf16[2,144,384]{2,1,0:T(8,128)(2,1)S(1)}, bf16[2,144,384]{2,1,0:T(8,128)(2,1)S(1)}, u32[]{:S(2)}, u32[]{:S(2)}) collective-permute-start(bf16[2,144,384]{2,1,0:T(8,128)(2,1)S(1)} %multiply_convert_fusion.1), channel_id=1, source_target_pairs={{0,8},{1,9},{2,10},{3,11},{4,12},{5,13},{6,14},{7,15},{8,0},{9,1},... | collective-permute-start | bytes 663560 | tf_op jit(solution)/shard_map/ppermute | solution.py:22
  26.3 1.6 %collective-permute-start.5 = (bf16[2,144,384]{2,1,0:T(8,128)(2,1)S(1)}, bf16[2,144,384]{2,1,0:T(8,128)(2,1)S(1)}, u32[]{:S(2)}, u32[]{:S(2)}) collective-permute-start(bf16[2,144,384]{2,1,0:T(8,128)(2,1)S(1)} %collective-permute-done.3.refs_4_), channel_id=1, source_target_pairs={{0,2},{1,3},{2,0},{3,1},{4,6},{5,7},{6,4},{7,5},{8,10},{9,11},{10,... | collective-permute-start | bytes 663560 | tf_op jit(solution)/shard_map/ppermute | solution.py:22
  28.3 0.7 %collective-permute-start.6 = (bf16[2,144,384]{2,1,0:T(8,128)(2,1)S(1)}, bf16[2,144,384]{2,1,0:T(8,128)(2,1)S(1)}, u32[]{:S(2)}, u32[]{:S(2)}) collective-permute-start(bf16[2,144,384]{2,1,0:T(8,128)(2,1)S(1)} %get-tuple-element.22), channel_id=1, source_target_pairs={{1,2},{2,1},{5,6},{6,5},{9,10},{10,9},{13,14},{14,13},{17,18},{18,... | collective-permute-start | bytes 663560 | tf_op jit(solution)/shard_map/ppermute | solution.py:30
  29.0 2.1 %collective-permute-start.7 = (bf16[2,144,384]{2,1,0:T(8,128)(2,1)S(1)}, bf16[2,144,384]{2,1,0:T(8,128)(2,1)S(1)}, u32[]{:S(2)}, u32[]{:S(2)}) collective-permute-start(bf16[2,144,384]{2,1,0:T(8,128)(2,1)S(1)} %multiply_convert_fusion), channel_id=1, source_target_pairs={{7,8},{8,7},{15,0},{0,15},{23,24},{24,23},{31,16},{16,31}} | collective-permute-start | bytes 663560 | tf_op jit(solution)/shard_map/ppermute | solution.py:30
  31.1 5.0 %collective-permute-done.5 = bf16[2,144,384]{2,1,0:T(8,128)(2,1)S(1)} collective-permute-done((bf16[2,144,384]{2,1,0:T(8,128)(2,1)S(1)}, bf16[2,144,384]{2,1,0:T(8,128)(2,1)S(1)}, u32[]{:S(2)}, u32[]{:S(2)}) %collective-permute-start.5) | collective-permute-done | bytes 221216 | tf_op jit(solution)/shard_map/ppermute | solution.py:22
  36.2 3.1 %collective-permute-done.4.refs_5_ = bf16[2,144,384]{2,1,0:T(8,128)(2,1)S(1)} collective-permute-done((bf16[2,144,384]{2,1,0:T(8,128)(2,1)S(1)}, bf16[2,144,384]{2,1,0:T(8,128)(2,1)S(1)}, u32[]{:S(2)}, u32[]{:S(2)}) %collective-permute-start.4) | collective-permute-done | bytes 221216 | tf_op jit(solution)/shard_map/ppermute | solution.py:22
  39.3 4.3 %collective-permute-start.9 = (bf16[2,144,384]{2,1,0:T(8,128)(2,1)S(1)}, bf16[2,144,384]{2,1,0:T(8,128)(2,1)S(1)}, u32[]{:S(2)}, u32[]{:S(2)}) collective-permute-start(bf16[2,144,384]{2,1,0:T(8,128)(2,1)S(1)} %collective-permute-done.4.refs_5_), channel_id=1, source_target_pairs={{0,2},{1,3},{2,0},{3,1},{4,6},{5,7},{6,4},{7,5},{8,10},{9,11},{10,... | collective-permute-start | bytes 663560 | tf_op jit(solution)/shard_map/ppermute | solution.py:22
  43.6 4.0 %fine.1.refs_0_ = bf16[2,3,4,144,256]{4,3,2,1,0:T(8,128)(2,1)S(1)} custom-call(s32[3]{0:T(128)S(1)} %pad_add_fusion.place.refs_0_, bf16[8,144,384]{2,1,0:T(8,128)(2,1)S(1)} %pad.7.refs_1_, bf16[8,144,384]{2,1,0:T(8,128)(2,1)S(1)} %pad.8.refs_2_, bf16[8,144,384]{2,1,0:T(8,128)(2,1)S(1)} %pad_maximum_fusion.refs_3_, ...), custom_call_target="tpu_custom_call" | custom-call | flops 800000000 | bytes 1000000 | tf_op jit(solution)/shard_map/fine/pallas_call | solution.py:244
  47.6 1.5 %collective-permute-done.9 = bf16[2,144,384]{2,1,0:T(8,128)(2,1)S(1)} collective-permute-done((bf16[2,144,384]{2,1,0:T(8,128)(2,1)S(1)}, bf16[2,144,384]{2,1,0:T(8,128)(2,1)S(1)}, u32[]{:S(2)}, u32[]{:S(2)}) %collective-permute-start.9) | collective-permute-done | bytes 221216 | tf_op jit(solution)/shard_map/ppermute | solution.py:22
  49.4 2.8 %third.1.refs_1_ = bf16[1,3,4,144,256]{4,3,2,1,0:T(8,128)(2,1)S(1)} custom-call(s32[3]{0:T(128)S(1)} %pad_add_fusion.place.refs_0_, bf16[8,144,384]{2,1,0:T(8,128)(2,1)S(1)} %pad.7.refs_1_, bf16[8,144,384]{2,1,0:T(8,128)(2,1)S(1)} %pad.8.refs_2_, bf16[8,144,384]{2,1,0:T(8,128)(2,1)S(1)} %pad_maximum_fusion.refs_3_, ...), custom_call_target="tpu_custom_call" | custom-call | flops 400000000 | bytes 1000000 | tf_op jit(solution)/shard_map/third/pallas_call | solution.py:244
  52.3 0.8 %vertical.1.refs_8_ = f32[3,144,1024]{2,1,0:T(8,128)S(1)} custom-call(bf16[5,3,144,256]{3,2,1,0:T(8,128)(2,1)S(1)} %choose.1.cov.refs_7_, bf16[2,3,4,144,256]{4,3,2,1,0:T(8,128)(2,1)S(1)} %fine.1.refs_0_, bf16[1,3,4,144,256]{4,3,2,1,0:T(8,128)(2,1)S(1)} %third.1.refs_1_), custom_call_target="tpu_custom_call" | custom-call | flops 500000000 | bytes 1000000 | tf_op jit(solution)/shard_map/vertical/pallas_call | solution.py:347
  53.2 0.9 %collective-permute-done.11 = bf16[4,144,384]{2,1,0:T(8,128)(2,1)S(1)} collective-permute-done((bf16[4,144,384]{2,1,0:T(8,128)(2,1)S(1)}, bf16[4,144,384]{2,1,0:T(8,128)(2,1)S(1)}, u32[]{:S(2)}, u32[]{:S(2)}) %collective-permute-start.11) | collective-permute-done | bytes 442400 | tf_op jit(solution)/shard_map/ppermute | solution.py:22
  54.3 4.9 %last.1 = bf16[8,144,384]{2,1,0:T(8,128)(2,1)S(1)} custom-call(s32[3]{0:T(128)S(1)} %pad_add_fusion.place.refs_0_, bf16[8,144,384]{2,1,0:T(8,128)(2,1)S(1)} %pad.7.refs_1_, bf16[8,144,384]{2,1,0:T(8,128)(2,1)S(1)} %pad.8.refs_2_, bf16[8,144,384]{2,1,0:T(8,128)(2,1)S(1)} %pad_maximum_fusion.refs_3_, bf16[8,144,384]{2,1,0:T(8,128)(2,1)S(1)} %pad_maximum_fusion.1.refs_4_, ...), custom_call_target="tpu_custom_call" | custom-call | flops 1000000000 | bytes 1000000 | tf_op jit(solution)/shard_map/last/pallas_call | solution.py:244
  59.3 1.1 %copy.12 = bf16[137,8,384]{2,1,0:T(8,128)(2,1)} copy(bf16[137,8,384]{2,0,1:T(8,128)(2,1)S(1)} %slice_bitcast_fusion) | data formatting | bytes 1683456 | tf_op jit(solution)/shard_map/transpose | solution.py:361
  (38 shorter events, 2.8 us)
Async XLA Ops:
  0.0 2.7 %collective-permute-start = (bf16[137,8,384]{2,1,0:T(8,128)(2,1)}, bf16[137,8,384]{2,1,0:T(8,128)(2,1)S(1)}, u32[]{:S(2)}, u32[]{:S(2)}) collective-permute-start(bf16[137,8,384]{2,1,0:T(8,128)(2,1)} %param.4), channel_id=1, source_target_pairs={{0,1},{1,0},{2,3},{3,2},{4,5},{5,4},{6,7},{7,6},{8,9},{9,8},{10,11... | collective-permute-start | bytes 2525192 | tf_op jit(solution)/shard_map/ppermute | solution.py:22
  2.8 3.3 %copy-start.2 = (s32[16,3]{0,1:T(4,128)S(1)}, s32[16,3]{0,1:T(4,128)}, u32[]{:S(2)}) copy-start(s32[16,3]{0,1:T(4,128)} %param.7) | copy-start | bytes 580
  3.1 13.4 %collective-permute-start.1 = (bf16[4,144,384]{2,1,0:T(8,128)(2,1)S(1)}, bf16[4,144,384]{2,1,0:T(8,128)(2,1)S(1)}, u32[]{:S(2)}, u32[]{:S(2)}) collective-permute-start(bf16[4,144,384]{2,1,0:T(8,128)(2,1)S(1)} %get-tuple-element.35), channel_id=1, source_target_pairs={{0,2},{1,3},{2,0},{3,1},{4,6},{5,7},{6,4},{7,5},{8,10},{9,11},{10,... | collective-permute-start | bytes 1327112 | tf_op jit(solution)/shard_map/ppermute | solution.py:22
  6.1 0.7 %copy-start.1 = (f32[5,25]{1,0:T(8,128)S(1)}, f32[5,25]{1,0:T(8,128)}, u32[]{:S(2)}) copy-start(f32[5,25]{1,0:T(8,128)} %taps.2) | copy-start | bytes 1504
  6.2 2.6 %copy-start = (bf16[5,16,137,137]{3,1,2,0:T(8,128)(2,1)S(1)}, bf16[5,16,137,137]{3,1,2,0:T(8,128)(2,1)}, u32[]{:S(2)}) copy-start(bf16[5,16,137,137]{3,1,2,0:T(8,128)(2,1)} %param.6) | copy-start | bytes 9009124
  16.6 7.5 %collective-permute-start.3 = (bf16[2,144,384]{2,1,0:T(8,128)(2,1)S(1)}, bf16[2,144,384]{2,1,0:T(8,128)(2,1)S(1)}, u32[]{:S(2)}, u32[]{:S(2)}) collective-permute-start(bf16[2,144,384]{2,1,0:T(8,128)(2,1)S(1)} %convert_element_type.45), channel_id=1, source_target_pairs={{0,4},{1,5},{2,6},{3,7},{4,0},{5,1},{6,2},{7,3},{8,12},{9,13},{10,... | collective-permute-start | bytes 663560 | tf_op jit(solution)/shard_map/ppermute | solution.py:22
  18.5 9.4 %collective-permute-start.2 = (bf16[4,144,384]{2,1,0:T(8,128)(2,1)S(1)}, bf16[4,144,384]{2,1,0:T(8,128)(2,1)S(1)}, u32[]{:S(2)}, u32[]{:S(2)}) collective-permute-start(bf16[4,144,384]{2,1,0:T(8,128)(2,1)S(1)} %collective-permute-done.1), channel_id=1, source_target_pairs={{0,1},{1,0},{2,3},{3,2},{4,5},{5,4},{6,7},{7,6},{8,9},{9,8},{10,11... | collective-permute-start | bytes 1327112 | tf_op jit(solution)/shard_map/ppermute | solution.py:22
  18.7 24.9 %collective-permute-start.10 = (bf16[4,144,384]{2,1,0:T(8,128)(2,1)S(1)}, bf16[4,144,384]{2,1,0:T(8,128)(2,1)S(1)}, u32[]{:S(2)}, u32[]{:S(2)}) collective-permute-start(bf16[4,144,384]{2,1,0:T(8,128)(2,1)S(1)} %pad_maximum_fusion.5), channel_id=1, source_target_pairs={{3,4},{4,3},{7,8},{8,7},{11,12},{12,11},{15,0},{0,15},{19,20},{20,... | collective-permute-start | bytes 1327112 | tf_op jit(solution)/shard_map/ppermute | solution.py:30
  24.2 15.1 %collective-permute-start.4 = (bf16[2,144,384]{2,1,0:T(8,128)(2,1)S(1)}, bf16[2,144,384]{2,1,0:T(8,128)(2,1)S(1)}, u32[]{:S(2)}, u32[]{:S(2)}) collective-permute-start(bf16[2,144,384]{2,1,0:T(8,128)(2,1)S(1)} %multiply_convert_fusion.1), channel_id=1, source_target_pairs={{0,8},{1,9},{2,10},{3,11},{4,12},{5,13},{6,14},{7,15},{8,0},{9,1},... | collective-permute-start | bytes 663560 | tf_op jit(solution)/shard_map/ppermute | solution.py:22
  26.3 9.8 %collective-permute-start.5 = (bf16[2,144,384]{2,1,0:T(8,128)(2,1)S(1)}, bf16[2,144,384]{2,1,0:T(8,128)(2,1)S(1)}, u32[]{:S(2)}, u32[]{:S(2)}) collective-permute-start(bf16[2,144,384]{2,1,0:T(8,128)(2,1)S(1)} %collective-permute-done.3.refs_4_), channel_id=1, source_target_pairs={{0,2},{1,3},{2,0},{3,1},{4,6},{5,7},{6,4},{7,5},{8,10},{9,11},{10,... | collective-permute-start | bytes 663560 | tf_op jit(solution)/shard_map/ppermute | solution.py:22
  28.3 11.0 %collective-permute-start.6 = (bf16[2,144,384]{2,1,0:T(8,128)(2,1)S(1)}, bf16[2,144,384]{2,1,0:T(8,128)(2,1)S(1)}, u32[]{:S(2)}, u32[]{:S(2)}) collective-permute-start(bf16[2,144,384]{2,1,0:T(8,128)(2,1)S(1)} %get-tuple-element.22), channel_id=1, source_target_pairs={{1,2},{2,1},{5,6},{6,5},{9,10},{10,9},{13,14},{14,13},{17,18},{18,... | collective-permute-start | bytes 663560 | tf_op jit(solution)/shard_map/ppermute | solution.py:30
  29.0 10.3 %collective-permute-start.7 = (bf16[2,144,384]{2,1,0:T(8,128)(2,1)S(1)}, bf16[2,144,384]{2,1,0:T(8,128)(2,1)S(1)}, u32[]{:S(2)}, u32[]{:S(2)}) collective-permute-start(bf16[2,144,384]{2,1,0:T(8,128)(2,1)S(1)} %multiply_convert_fusion), channel_id=1, source_target_pairs={{7,8},{8,7},{15,0},{0,15},{23,24},{24,23},{31,16},{16,31}} | collective-permute-start | bytes 663560 | tf_op jit(solution)/shard_map/ppermute | solution.py:30
  39.3 9.8 %collective-permute-start.9 = (bf16[2,144,384]{2,1,0:T(8,128)(2,1)S(1)}, bf16[2,144,384]{2,1,0:T(8,128)(2,1)S(1)}, u32[]{:S(2)}, u32[]{:S(2)}) collective-permute-start(bf16[2,144,384]{2,1,0:T(8,128)(2,1)S(1)} %collective-permute-done.4.refs_5_), channel_id=1, source_target_pairs={{0,2},{1,3},{2,0},{3,1},{4,6},{5,7},{6,4},{7,5},{8,10},{9,11},{10,... | collective-permute-start | bytes 663560 | tf_op jit(solution)/shard_map/ppermute | solution.py:22
  43.6 5.6 %collective-permute-start.8 = (bf16[4,144,384]{2,1,0:T(8,128)(2,1)S(1)}, bf16[4,144,384]{2,1,0:T(8,128)(2,1)S(1)}, u32[]{:S(2)}, u32[]{:S(2)}) collective-permute-start(bf16[4,144,384]{2,1,0:T(8,128)(2,1)S(1)} %pad_maximum_fusion.3), channel_id=1, source_target_pairs={{0,1},{1,0},{2,3},{3,2},{4,5},{5,4},{6,7},{7,6},{8,9},{9,8},{10,11... | collective-permute-start | bytes 1327112 | tf_op jit(solution)/shard_map/ppermute | solution.py:22
  52.2 1.9 %collective-permute-start.11 = (bf16[4,144,384]{2,1,0:T(8,128)(2,1)S(1)}, bf16[4,144,384]{2,1,0:T(8,128)(2,1)S(1)}, u32[]{:S(2)}, u32[]{:S(2)}) collective-permute-start(bf16[4,144,384]{2,1,0:T(8,128)(2,1)S(1)} %pad_maximum_fusion.4), channel_id=1, source_target_pairs={{0,1},{1,0},{2,3},{3,2},{4,5},{5,4},{6,7},{7,6},{8,9},{9,8},{10,11... | collective-permute-start | bytes 1327112 | tf_op jit(solution)/shard_map/ppermute | solution.py:22

commit v5 on v4

--- a/solution.py
+++ b/solution.py
@@ -169,7 +169,8 @@
 
 def last_kernel(ks, lons, blocks, halos, *refs):
     info, s0, r, h, weights, refs = split_refs(refs, ks, halos)
-    cov, acc, out, bands, ends, done = refs
+    cov, acc, out, bands, ends, done, turned = refs
+    levels = out.shape[0]
     rows = s0.shape[1]
     pairs = lons // 2
 
@@ -183,10 +184,11 @@
             total = acc[block, :, at]
             for i, k in enumerate(ks):
                 total = total + jnp.dot(cov[k, block, :, :rows], done[i, block, pair], preferred_element_type=F32)
-            total = total.astype(BF16)
             for half in range(2):
-                out[2 * pair + half, :, block * LANES:(block + 1) * LANES] = (
+                turned[block, pl.ds(2 * pair + half, rows, stride=lons), :] = (
                     total[:, half * LANES:(half + 1) * LANES])
+        out[:, :, block * LANES:(block + 1) * LANES] = (
+            turned[block].reshape(rows, lons, LANES)[:levels].astype(BF16))
 
 
 def vertical_kernel(lons, blocks, cov, *refs):
@@ -226,7 +228,7 @@
     return pl.CostEstimate(flops=int(flops), bytes_accessed=int(data), transcendentals=0)
 
 
-def filter_part(ks, info, s0, r, h, weights, name, flops, cov=None, acc=None):
+def filter_part(ks, info, s0, r, h, weights, name, flops, cov=None, acc=None, levels=None):
     lons, rows, lat = s0.shape
     blocks, pairs = lat // LANES, lons // 2
     halos = [level for level in range(ks[0], min(ks[-1] + 1, LEVELS) + 1) if level in h]
@@ -240,7 +242,8 @@
         kernel = last_kernel
         operands += [cov, acc]
         scratch.append(pltpu.VMEM((len(ks), blocks, pairs, rows, 2 * LANES), BF16))
-        shape = jax.ShapeDtypeStruct((lons, rows, lat), BF16)
+        scratch.append(pltpu.VMEM((blocks, rows * lons, LANES), F32))
+        shape = jax.ShapeDtypeStruct((levels, lons, lat), BF16)
     return pl.pallas_call(
         functools.partial(kernel, ks, lons, blocks, halos),
         out_shape=shape,
@@ -357,8 +360,8 @@
     if count > 1 << LEVELS:
         s4_edge = mean(s3_edge, edge(r3))
         h[4] = outer_swap(s4_edge.astype(BF16), 3, count)
-    out = filter_part((3, 4), info, s0, (r0, r1, r2, r3), h, weights, "last", 1e9, chosen, acc)
-    return jnp.transpose(out[:, :levels], (1, 0, 2))
+    out = filter_part((3, 4), info, s0, (r0, r1, r2, r3), h, weights, "last", 1e9, chosen, acc, levels)
+    return out
 
 
 def solution(mesh):

time: 60.7 us -> 60.6 us (level)
  local copies, waits for them, and re-layouts: 3.8 us -> 2.64 us
  Pallas kernels: 16.7 us -> 17.8 us
    transpose x2 -> x0, local copies, waits for them, and re-layouts: 1.16 us -> none  [on_device(): return jnp.transpose(out[:, :levels], (1, 0, 2))]
    pallas_call x3, Pallas kernels: 11.7 us -> 12.8 us  [filter_part(): pl.pallas_call(functools.partial(kernel, ks, lons, blocks, halos), out_sh...]
where the time goes in v5:
time: 60.6 us; the launch traced here: 60.3 us
  starting transfers between devices  21.5 us (35%)
  Pallas kernels  17.8 us (29%)
  waiting for transfers between devices  16.3 us (27%)
  local copies, waits for them, and re-layouts  2.64 us (4%)
  other arithmetic  1.75 us (3%)
    ppermute x9, waiting for transfers between devices, swap(): return lax.ppermute(field, 'lon', [(t, t ^ 1 << bit) for t in range(count)])  16.3 us
    ppermute x9, starting transfers between devices, swap(): return lax.ppermute(field, 'lon', [(t, t ^ 1 << bit) for t in range(count)])  13.3 us
    pallas_call x3, Pallas kernels, filter_part(): pl.pallas_call(functools.partial(kernel, ks, lons, blocks, halos), out_sh...  12.8 us
    ppermute x3, starting transfers between devices, outer_swap(): return lax.ppermute(edge, 'lon', route)  8.2 us
    pallas_call x1, Pallas kernels, on_device(): pl.pallas_call(functools.partial(choose_kernel, levels, rows, blocks), ou...  2.68 us
    unnamed x8, local copies, waits for them, and re-layouts  2.34 us
    pallas_call x1, Pallas kernels, on_device(): pl.pallas_call(prep_kernel, out_shape=jax.ShapeDtypeStruct((BANDS, 7 * LA...  1.5 us
  transfers between devices with their start and end apart: 12, of which 6 were waited for; matrix products, arithmetic and copies ran while one was open for 4% of the time, Pallas kernels for 15%

profile of v5, /device:TPU:0, one launch (start us, length us, event | category | flops | bytes accessed | tf_op | source)
XLA Modules:
  0.0 60.3 jit_solution(10154743719120734731)
XLA Ops:
  0.0 0.5 collective-permute-start
  0.5 1.3 %copy.14 = bf16[137,8,384]{2,0,1:T(8,128)(2,1)S(1)} copy(bf16[137,8,384]{2,1,0:T(8,128)(2,1)} %param.4) | data formatting | bytes 1683456 | tf_op args[0]
  1.8 0.9 %collective-permute-done = bf16[137,8,384]{2,1,0:T(8,128)(2,1)S(1)} collective-permute-done((bf16[137,8,384]{2,1,0:T(8,128)(2,1)}, bf16[137,8,384]{2,1,0:T(8,128)(2,1)S(1)}, u32[]{:S(2)}, u32[]{:S(2)}) %collective-permute-start) | collective-permute-done | bytes 841760 | tf_op jit(solution)/shard_map/ppermute | solution.py:22
  3.1 2.9 %collective-permute-start.1 = (bf16[4,144,384]{2,1,0:T(8,128)(2,1)S(1)}, bf16[4,144,384]{2,1,0:T(8,128)(2,1)S(1)}, u32[]{:S(2)}, u32[]{:S(2)}) collective-permute-start(bf16[4,144,384]{2,1,0:T(8,128)(2,1)S(1)} %get-tuple-element.35), channel_id=1, source_target_pairs={{0,2},{1,3},{2,0},{3,1},{4,6},{5,7},{6,4},{7,5},{8,10},{9,11},{10,... | collective-permute-start | bytes 1327112 | tf_op jit(solution)/shard_map/ppermute | solution.py:22
  6.4 0.5 copy-done.1
  6.8 1.5 %taps.1.refs_8_.refs_7_.refs_6_ = bf16[5,896,256]{2,1,0:T(8,128)(2,1)S(1)} custom-call(f32[5,25]{1,0:T(8,128)S(1)} %copy-done.1), custom_call_target="tpu_custom_call" | custom-call | flops 1500000000 | bytes 1000000 | tf_op jit(solution)/shard_map/taps/pallas_call | solution.py:305
  8.3 0.5 copy-done
  8.8 2.7 %choose.1.cov.refs_7_ = bf16[5,3,144,256]{3,2,1,0:T(8,128)(2,1)S(1)} custom-call(s32[3]{0:T(128)S(1)} %pad_add_fusion.place.refs_0_, s32[16,3]{1,0:T(8,128)S(1)} %copy.10.region, bf16[5,137,16,137]{3,2,1,0:T(8,128)(2,1)S(1)} %bitcast.10), custom_call_target="tpu_custom_call" | custom-call | flops 3000000000 | bytes 6000000 | tf_op jit(solution)/shard_map/choose/pallas_call | solution.py:316
  11.5 4.9 %collective-permute-done.1 = bf16[4,144,384]{2,1,0:T(8,128)(2,1)S(1)} collective-permute-done((bf16[4,144,384]{2,1,0:T(8,128)(2,1)S(1)}, bf16[4,144,384]{2,1,0:T(8,128)(2,1)S(1)}, u32[]{:S(2)}, u32[]{:S(2)}) %collective-permute-start.1) | collective-permute-done | bytes 442400 | tf_op jit(solution)/shard_map/ppermute | solution.py:22
  16.6 1.9 %collective-permute-start.3 = (bf16[2,144,384]{2,1,0:T(8,128)(2,1)S(1)}, bf16[2,144,384]{2,1,0:T(8,128)(2,1)S(1)}, u32[]{:S(2)}, u32[]{:S(2)}) collective-permute-start(bf16[2,144,384]{2,1,0:T(8,128)(2,1)S(1)} %convert_element_type.45), channel_id=1, source_target_pairs={{0,4},{1,5},{2,6},{3,7},{4,0},{5,1},{6,2},{7,3},{8,12},{9,13},{10,... | collective-permute-start | bytes 663560 | tf_op jit(solution)/shard_map/ppermute | solution.py:22
  18.7 5.4 %collective-permute-start.10 = (bf16[4,144,384]{2,1,0:T(8,128)(2,1)S(1)}, bf16[4,144,384]{2,1,0:T(8,128)(2,1)S(1)}, u32[]{:S(2)}, u32[]{:S(2)}) collective-permute-start(bf16[4,144,384]{2,1,0:T(8,128)(2,1)S(1)} %pad_maximum_fusion.5), channel_id=1, source_target_pairs={{3,4},{4,3},{7,8},{8,7},{11,12},{12,11},{15,0},{0,15},{19,20},{20,... | collective-permute-start | bytes 1327112 | tf_op jit(solution)/shard_map/ppermute | solution.py:30
  24.2 2.1 %collective-permute-start.4 = (bf16[2,144,384]{2,1,0:T(8,128)(2,1)S(1)}, bf16[2,144,384]{2,1,0:T(8,128)(2,1)S(1)}, u32[]{:S(2)}, u32[]{:S(2)}) collective-permute-start(bf16[2,144,384]{2,1,0:T(8,128)(2,1)S(1)} %multiply_convert_fusion.1), channel_id=1, source_target_pairs={{0,8},{1,9},{2,10},{3,11},{4,12},{5,13},{6,14},{7,15},{8,0},{9,1},... | collective-permute-start | bytes 663560 | tf_op jit(solution)/shard_map/ppermute | solution.py:22
  26.3 1.6 %collective-permute-start.5 = (bf16[2,144,384]{2,1,0:T(8,128)(2,1)S(1)}, bf16[2,144,384]{2,1,0:T(8,128)(2,1)S(1)}, u32[]{:S(2)}, u32[]{:S(2)}) collective-permute-start(bf16[2,144,384]{2,1,0:T(8,128)(2,1)S(1)} %collective-permute-done.3.refs_4_), channel_id=1, source_target_pairs={{0,2},{1,3},{2,0},{3,1},{4,6},{5,7},{6,4},{7,5},{8,10},{9,11},{10,... | collective-permute-start | bytes 663560 | tf_op jit(solution)/shard_map/ppermute | solution.py:22
  28.3 0.7 %collective-permute-start.6 = (bf16[2,144,384]{2,1,0:T(8,128)(2,1)S(1)}, bf16[2,144,384]{2,1,0:T(8,128)(2,1)S(1)}, u32[]{:S(2)}, u32[]{:S(2)}) collective-permute-start(bf16[2,144,384]{2,1,0:T(8,128)(2,1)S(1)} %get-tuple-element.22), channel_id=1, source_target_pairs={{1,2},{2,1},{5,6},{6,5},{9,10},{10,9},{13,14},{14,13},{17,18},{18,... | collective-permute-start | bytes 663560 | tf_op jit(solution)/shard_map/ppermute | solution.py:30
  29.0 2.1 %collective-permute-start.7 = (bf16[2,144,384]{2,1,0:T(8,128)(2,1)S(1)}, bf16[2,144,384]{2,1,0:T(8,128)(2,1)S(1)}, u32[]{:S(2)}, u32[]{:S(2)}) collective-permute-start(bf16[2,144,384]{2,1,0:T(8,128)(2,1)S(1)} %multiply_convert_fusion), channel_id=1, source_target_pairs={{7,8},{8,7},{15,0},{0,15},{23,24},{24,23},{31,16},{16,31}} | collective-permute-start | bytes 663560 | tf_op jit(solution)/shard_map/ppermute | solution.py:30
  31.1 5.0 %collective-permute-done.5 = bf16[2,144,384]{2,1,0:T(8,128)(2,1)S(1)} collective-permute-done((bf16[2,144,384]{2,1,0:T(8,128)(2,1)S(1)}, bf16[2,144,384]{2,1,0:T(8,128)(2,1)S(1)}, u32[]{:S(2)}, u32[]{:S(2)}) %collective-permute-start.5) | collective-permute-done | bytes 221216 | tf_op jit(solution)/shard_map/ppermute | solution.py:22
  36.2 3.1 %collective-permute-done.4.refs_5_ = bf16[2,144,384]{2,1,0:T(8,128)(2,1)S(1)} collective-permute-done((bf16[2,144,384]{2,1,0:T(8,128)(2,1)S(1)}, bf16[2,144,384]{2,1,0:T(8,128)(2,1)S(1)}, u32[]{:S(2)}, u32[]{:S(2)}) %collective-permute-start.4) | collective-permute-done | bytes 221216 | tf_op jit(solution)/shard_map/ppermute | solution.py:22
  39.3 4.3 %collective-permute-start.9 = (bf16[2,144,384]{2,1,0:T(8,128)(2,1)S(1)}, bf16[2,144,384]{2,1,0:T(8,128)(2,1)S(1)}, u32[]{:S(2)}, u32[]{:S(2)}) collective-permute-start(bf16[2,144,384]{2,1,0:T(8,128)(2,1)S(1)} %collective-permute-done.4.refs_5_), channel_id=1, source_target_pairs={{0,2},{1,3},{2,0},{3,1},{4,6},{5,7},{6,4},{7,5},{8,10},{9,11},{10,... | collective-permute-start | bytes 663560 | tf_op jit(solution)/shard_map/ppermute | solution.py:22
  43.6 4.0 %fine.1.refs_0_ = bf16[2,3,4,144,256]{4,3,2,1,0:T(8,128)(2,1)S(1)} custom-call(s32[3]{0:T(128)S(1)} %pad_add_fusion.place.refs_0_, bf16[8,144,384]{2,1,0:T(8,128)(2,1)S(1)} %pad.7.refs_1_, bf16[8,144,384]{2,1,0:T(8,128)(2,1)S(1)} %pad.8.refs_2_, bf16[8,144,384]{2,1,0:T(8,128)(2,1)S(1)} %pad_maximum_fusion.refs_3_, ...), custom_call_target="tpu_custom_call" | custom-call | flops 800000000 | bytes 1000000 | tf_op jit(solution)/shard_map/fine/pallas_call | solution.py:247
  47.6 1.5 %collective-permute-done.9 = bf16[2,144,384]{2,1,0:T(8,128)(2,1)S(1)} collective-permute-done((bf16[2,144,384]{2,1,0:T(8,128)(2,1)S(1)}, bf16[2,144,384]{2,1,0:T(8,128)(2,1)S(1)}, u32[]{:S(2)}, u32[]{:S(2)}) %collective-permute-start.9) | collective-permute-done | bytes 221216 | tf_op jit(solution)/shard_map/ppermute | solution.py:22
  49.4 2.8 %third.1.refs_1_ = bf16[1,3,4,144,256]{4,3,2,1,0:T(8,128)(2,1)S(1)} custom-call(s32[3]{0:T(128)S(1)} %pad_add_fusion.place.refs_0_, bf16[8,144,384]{2,1,0:T(8,128)(2,1)S(1)} %pad.7.refs_1_, bf16[8,144,384]{2,1,0:T(8,128)(2,1)S(1)} %pad.8.refs_2_, bf16[8,144,384]{2,1,0:T(8,128)(2,1)S(1)} %pad_maximum_fusion.refs_3_, ...), custom_call_target="tpu_custom_call" | custom-call | flops 400000000 | bytes 1000000 | tf_op jit(solution)/shard_map/third/pallas_call | solution.py:247
  52.3 0.8 %vertical.1.refs_8_ = f32[3,144,1024]{2,1,0:T(8,128)S(1)} custom-call(bf16[5,3,144,256]{3,2,1,0:T(8,128)(2,1)S(1)} %choose.1.cov.refs_7_, bf16[2,3,4,144,256]{4,3,2,1,0:T(8,128)(2,1)S(1)} %fine.1.refs_0_, bf16[1,3,4,144,256]{4,3,2,1,0:T(8,128)(2,1)S(1)} %third.1.refs_1_), custom_call_target="tpu_custom_call" | custom-call | flops 500000000 | bytes 1000000 | tf_op jit(solution)/shard_map/vertical/pallas_call | solution.py:350
  53.2 0.9 %collective-permute-done.11 = bf16[4,144,384]{2,1,0:T(8,128)(2,1)S(1)} collective-permute-done((bf16[4,144,384]{2,1,0:T(8,128)(2,1)S(1)}, bf16[4,144,384]{2,1,0:T(8,128)(2,1)S(1)}, u32[]{:S(2)}, u32[]{:S(2)}) %collective-permute-start.11) | collective-permute-done | bytes 442400 | tf_op jit(solution)/shard_map/ppermute | solution.py:22
  54.3 6.0 %last.1 = bf16[137,8,384]{2,1,0:T(8,128)(2,1)} custom-call(s32[3]{0:T(128)S(1)} %pad_add_fusion.place.refs_0_, bf16[8,144,384]{2,1,0:T(8,128)(2,1)S(1)} %pad.7.refs_1_, bf16[8,144,384]{2,1,0:T(8,128)(2,1)S(1)} %pad.8.refs_2_, bf16[8,144,384]{2,1,0:T(8,128)(2,1)S(1)} %pad_maximum_fusion.refs_3_, bf16[8,144,384]{2,1,0:T(8,128)(2,1)S(1)} %pad_maximum_fusion.1.refs_4_, ...), custom_call_target="tpu_custom_call" | custom-call | flops 1000000000 | bytes 1000000 | tf_op jit(solution)/shard_map/last/pallas_call | solution.py:247
  (36 shorter events, 2.2 us)
Async XLA Ops:
  0.0 2.7 %collective-permute-start = (bf16[137,8,384]{2,1,0:T(8,128)(2,1)}, bf16[137,8,384]{2,1,0:T(8,128)(2,1)S(1)}, u32[]{:S(2)}, u32[]{:S(2)}) collective-permute-start(bf16[137,8,384]{2,1,0:T(8,128)(2,1)} %param.4), channel_id=1, source_target_pairs={{0,1},{1,0},{2,3},{3,2},{4,5},{5,4},{6,7},{7,6},{8,9},{9,8},{10,11... | collective-permute-start | bytes 2525192 | tf_op jit(solution)/shard_map/ppermute | solution.py:22
  2.8 3.3 %copy-start.2 = (s32[16,3]{0,1:T(4,128)S(1)}, s32[16,3]{0,1:T(4,128)}, u32[]{:S(2)}) copy-start(s32[16,3]{0,1:T(4,128)} %param.7) | copy-start | bytes 580
  3.1 13.4 %collective-permute-start.1 = (bf16[4,144,384]{2,1,0:T(8,128)(2,1)S(1)}, bf16[4,144,384]{2,1,0:T(8,128)(2,1)S(1)}, u32[]{:S(2)}, u32[]{:S(2)}) collective-permute-start(bf16[4,144,384]{2,1,0:T(8,128)(2,1)S(1)} %get-tuple-element.35), channel_id=1, source_target_pairs={{0,2},{1,3},{2,0},{3,1},{4,6},{5,7},{6,4},{7,5},{8,10},{9,11},{10,... | collective-permute-start | bytes 1327112 | tf_op jit(solution)/shard_map/ppermute | solution.py:22
  6.1 0.7 %copy-start.1 = (f32[5,25]{1,0:T(8,128)S(1)}, f32[5,25]{1,0:T(8,128)}, u32[]{:S(2)}) copy-start(f32[5,25]{1,0:T(8,128)} %taps.2) | copy-start | bytes 1504
  6.2 2.6 %copy-start = (bf16[5,16,137,137]{3,1,2,0:T(8,128)(2,1)S(1)}, bf16[5,16,137,137]{3,1,2,0:T(8,128)(2,1)}, u32[]{:S(2)}) copy-start(bf16[5,16,137,137]{3,1,2,0:T(8,128)(2,1)} %param.6) | copy-start | bytes 9009124
  16.6 7.5 %collective-permute-start.3 = (bf16[2,144,384]{2,1,0:T(8,128)(2,1)S(1)}, bf16[2,144,384]{2,1,0:T(8,128)(2,1)S(1)}, u32[]{:S(2)}, u32[]{:S(2)}) collective-permute-start(bf16[2,144,384]{2,1,0:T(8,128)(2,1)S(1)} %convert_element_type.45), channel_id=1, source_target_pairs={{0,4},{1,5},{2,6},{3,7},{4,0},{5,1},{6,2},{7,3},{8,12},{9,13},{10,... | collective-permute-start | bytes 663560 | tf_op jit(solution)/shard_map/ppermute | solution.py:22
  18.5 9.4 %collective-permute-start.2 = (bf16[4,144,384]{2,1,0:T(8,128)(2,1)S(1)}, bf16[4,144,384]{2,1,0:T(8,128)(2,1)S(1)}, u32[]{:S(2)}, u32[]{:S(2)}) collective-permute-start(bf16[4,144,384]{2,1,0:T(8,128)(2,1)S(1)} %collective-permute-done.1), channel_id=1, source_target_pairs={{0,1},{1,0},{2,3},{3,2},{4,5},{5,4},{6,7},{7,6},{8,9},{9,8},{10,11... | collective-permute-start | bytes 1327112 | tf_op jit(solution)/shard_map/ppermute | solution.py:22
  18.7 24.9 %collective-permute-start.10 = (bf16[4,144,384]{2,1,0:T(8,128)(2,1)S(1)}, bf16[4,144,384]{2,1,0:T(8,128)(2,1)S(1)}, u32[]{:S(2)}, u32[]{:S(2)}) collective-permute-start(bf16[4,144,384]{2,1,0:T(8,128)(2,1)S(1)} %pad_maximum_fusion.5), channel_id=1, source_target_pairs={{3,4},{4,3},{7,8},{8,7},{11,12},{12,11},{15,0},{0,15},{19,20},{20,... | collective-permute-start | bytes 1327112 | tf_op jit(solution)/shard_map/ppermute | solution.py:30
  24.2 15.1 %collective-permute-start.4 = (bf16[2,144,384]{2,1,0:T(8,128)(2,1)S(1)}, bf16[2,144,384]{2,1,0:T(8,128)(2,1)S(1)}, u32[]{:S(2)}, u32[]{:S(2)}) collective-permute-start(bf16[2,144,384]{2,1,0:T(8,128)(2,1)S(1)} %multiply_convert_fusion.1), channel_id=1, source_target_pairs={{0,8},{1,9},{2,10},{3,11},{4,12},{5,13},{6,14},{7,15},{8,0},{9,1},... | collective-permute-start | bytes 663560 | tf_op jit(solution)/shard_map/ppermute | solution.py:22
  26.3 9.8 %collective-permute-start.5 = (bf16[2,144,384]{2,1,0:T(8,128)(2,1)S(1)}, bf16[2,144,384]{2,1,0:T(8,128)(2,1)S(1)}, u32[]{:S(2)}, u32[]{:S(2)}) collective-permute-start(bf16[2,144,384]{2,1,0:T(8,128)(2,1)S(1)} %collective-permute-done.3.refs_4_), channel_id=1, source_target_pairs={{0,2},{1,3},{2,0},{3,1},{4,6},{5,7},{6,4},{7,5},{8,10},{9,11},{10,... | collective-permute-start | bytes 663560 | tf_op jit(solution)/shard_map/ppermute | solution.py:22
  28.3 11.0 %collective-permute-start.6 = (bf16[2,144,384]{2,1,0:T(8,128)(2,1)S(1)}, bf16[2,144,384]{2,1,0:T(8,128)(2,1)S(1)}, u32[]{:S(2)}, u32[]{:S(2)}) collective-permute-start(bf16[2,144,384]{2,1,0:T(8,128)(2,1)S(1)} %get-tuple-element.22), channel_id=1, source_target_pairs={{1,2},{2,1},{5,6},{6,5},{9,10},{10,9},{13,14},{14,13},{17,18},{18,... | collective-permute-start | bytes 663560 | tf_op jit(solution)/shard_map/ppermute | solution.py:30
  29.0 10.3 %collective-permute-start.7 = (bf16[2,144,384]{2,1,0:T(8,128)(2,1)S(1)}, bf16[2,144,384]{2,1,0:T(8,128)(2,1)S(1)}, u32[]{:S(2)}, u32[]{:S(2)}) collective-permute-start(bf16[2,144,384]{2,1,0:T(8,128)(2,1)S(1)} %multiply_convert_fusion), channel_id=1, source_target_pairs={{7,8},{8,7},{15,0},{0,15},{23,24},{24,23},{31,16},{16,31}} | collective-permute-start | bytes 663560 | tf_op jit(solution)/shard_map/ppermute | solution.py:30
  39.3 9.8 %collective-permute-start.9 = (bf16[2,144,384]{2,1,0:T(8,128)(2,1)S(1)}, bf16[2,144,384]{2,1,0:T(8,128)(2,1)S(1)}, u32[]{:S(2)}, u32[]{:S(2)}) collective-permute-start(bf16[2,144,384]{2,1,0:T(8,128)(2,1)S(1)} %collective-permute-done.4.refs_5_), channel_id=1, source_target_pairs={{0,2},{1,3},{2,0},{3,1},{4,6},{5,7},{6,4},{7,5},{8,10},{9,11},{10,... | collective-permute-start | bytes 663560 | tf_op jit(solution)/shard_map/ppermute | solution.py:22
  43.6 5.6 %collective-permute-start.8 = (bf16[4,144,384]{2,1,0:T(8,128)(2,1)S(1)}, bf16[4,144,384]{2,1,0:T(8,128)(2,1)S(1)}, u32[]{:S(2)}, u32[]{:S(2)}) collective-permute-start(bf16[4,144,384]{2,1,0:T(8,128)(2,1)S(1)} %pad_maximum_fusion.3), channel_id=1, source_target_pairs={{0,1},{1,0},{2,3},{3,2},{4,5},{5,4},{6,7},{7,6},{8,9},{9,8},{10,11... | collective-permute-start | bytes 1327112 | tf_op jit(solution)/shard_map/ppermute | solution.py:22
  52.2 1.9 %collective-permute-start.11 = (bf16[4,144,384]{2,1,0:T(8,128)(2,1)S(1)}, bf16[4,144,384]{2,1,0:T(8,128)(2,1)S(1)}, u32[]{:S(2)}, u32[]{:S(2)}) collective-permute-start(bf16[4,144,384]{2,1,0:T(8,128)(2,1)S(1)} %pad_maximum_fusion.4), channel_id=1, source_target_pairs={{0,1},{1,0},{2,3},{3,2},{4,5},{5,4},{6,7},{7,6},{8,9},{9,8},{10,11... | collective-permute-start | bytes 1327112 | tf_op jit(solution)/shard_map/ppermute | solution.py:22
